TPU v7x, 128 devices: a whole 4x4x4 slice. The times are simulated.
128 devices in a mesh: seq: 4 (over y), head: 8 (over x, z_hi), dp: 4 (over z_lo, core).
Axes of the slice: x: 4, y: 4, z: 4 (z_hi: 2, z_lo: 2; z = z_hi * 2 + z_lo), core: 2. Of those that a mesh axis runs over, the one named last changes fastest.
Arguments:
- tokens: bfloat16 [8192, 3072], P(('dp', 'seq', 'head')), parts along dimension 0, may hold values from -6 to 6
- norm_gain: float32 [2, 3072], replicated, may hold values from 0.5 to 1.5
- qkv_weight: bfloat16 [2, 3072, 9216], P(None, None, 'head'), may hold values from -0.109375 to 0.109375
- rate_weight: bfloat16 [2, 3072, 48], P(None, None, 'head'), may hold values from -0.109375 to 0.109375
- rate_base: float32 [2, 48], P(None, 'head'), may hold values from 0.003 to 0.03
- fast_first: float32 [2, 48, 64, 256], P(None, 'head'), may hold values from -0.75 to 0.75
- fast_second: float32 [2, 48, 64, 256], P(None, 'head'), may hold values from -0.375 to 0.375
- inner_gain: float32 [2, 48, 64], P(None, 'head'), may hold values from 0.1 to 1.9
- out_weight: bfloat16 [2, 3072, 3072], P(None, 'head'), may hold values from -0.109375 to 0.109375
Outputs:
- stream_out: bfloat16 [8192, 3072], P(('dp', 'seq', 'head')), parts along dimension 0
There are 4 independent parts, one for each index of `dp`. A program takes and returns all parts, laid end to end along the dimension named above; an argument that names none is the same for every part. Nothing has to cross between parts.
All inputs are finite; a program needn't handle non-finite values.
Results may differ from a plain program's by a relative error of at most 0.027.
Values may be sent and summed in bfloat16 or wider, within the bound.
No kernel may reach another device: no remote copies, remote signals or barrier semaphores. Data moves between devices by JAX's collectives and lax.ppermute only.
A program may use at most 192 MiB of HBM per device.

v0:
```python
from functools import partial

import jax
import jax.numpy as jnp
from jax import lax
from jax.sharding import PartitionSpec as P

MB = 64


def as_sent(array):

    def short(part):
        return part.astype(jnp.bfloat16) if part.dtype == jnp.float32 else part

    return jax.tree.map(short, array)


def from_behind(block, axis, distance):
    devices = range(lax.axis_size(axis))
    route = [(i - distance, i) for i in devices if i - distance in devices]
    return lax.ppermute(block, axis, route)


def narrow_product(form, left, right):
    return jnp.einsum(
        form,
        left.astype(jnp.bfloat16),
        right.astype(jnp.bfloat16),
        preferred_element_type=jnp.float32,
    )


def inner_apply(first_mat, second_mat, gain_rows, inputs):
    hidden = jax.nn.gelu(narrow_product("hnd,hdf->hnf", inputs, first_mat))
    result = narrow_product("hnf,hdf->hnd", hidden, second_mat)
    centre = result - jnp.mean(result, axis=-1, keepdims=True)
    spread = jnp.mean(centre * centre, axis=-1, keepdims=True)
    return centre * lax.rsqrt(spread + 1e-05) * gain_rows[:, None, :]


def inner_loss(weights, gain_rows, key_rows, target_rows, gate_rates):
    predicted = inner_apply(weights[0], weights[1], gain_rows, key_rows)
    differ = predicted - target_rows
    return jnp.sum(gate_rates[..., None] * differ * differ) * (0.5 / key_rows.shape[1])


def update(gain_rows, weights, batch_rows):
    queries, key_rows, value_rows, gate_rates = batch_rows
    gradient = jax.grad(inner_loss)(weights, gain_rows, key_rows, value_rows - key_rows, gate_rates)
    renewed = (
        weights[0] - gradient[0].astype(jnp.float32),
        weights[1] - gradient[1].astype(jnp.float32),
    )
    return (renewed, queries + inner_apply(renewed[0], renewed[1], gain_rows, queries))


def project_inputs(stream, gain_vector, qkv_cols, rate_cols, rate_scale):
    widened = stream.astype(jnp.float32)
    mean_square = jnp.mean(widened * widened, axis=-1, keepdims=True)
    normed = (widened * lax.rsqrt(mean_square + 1e-06) * gain_vector).astype(jnp.bfloat16)
    packed = jnp.dot(normed, qkv_cols, preferred_element_type=jnp.float32)
    token_count = stream.shape[0]
    head_count = rate_cols.shape[1]
    packed = packed.reshape(token_count // MB, MB, head_count, 3, -1).transpose(0, 2, 3, 1, 4)
    gate_rates = rate_scale[None, :] * jax.nn.sigmoid(
        jnp.dot(normed, rate_cols, preferred_element_type=jnp.float32)
    )
    gate_rates = gate_rates.reshape(token_count // MB, MB, head_count).transpose(0, 2, 1)
    return (packed[:, :, 0], packed[:, :, 1], packed[:, :, 2], gate_rates)


def run_chain(start_state, batches, gain_rows):
    final_state, outputs = lax.scan(partial(update, gain_rows), start_state, batches)
    block_count, head_count, batch_size, head_size = outputs.shape
    flat = outputs.transpose(0, 2, 1, 3).reshape(block_count * batch_size, head_count * head_size)
    return (final_state, flat)


def widen(stream):
    return lax.all_gather(stream, "head", axis=0, tiled=True)


def hand_over(final_state):
    return from_behind((as_sent(final_state[0]), as_sent(final_state[1])), "seq", 1)


def body(
    tokens,
    norm_gain,
    qkv_weight,
    rate_weight,
    rate_base,
    fast_first,
    fast_second,
    inner_gain,
    out_weight,
):
    seq_count = lax.axis_size("seq")
    seq_place = lax.axis_index("seq")
    layer_count = norm_gain.shape[0]
    stream = tokens
    for layer_index in range(layer_count):
        whole_rows = widen(stream)
        batches = project_inputs(
            whole_rows,
            norm_gain[layer_index],
            qkv_weight[layer_index],
            rate_weight[layer_index],
            rate_base[layer_index],
        )
        initial = (fast_first[layer_index], fast_second[layer_index])
        start_state = initial
        for round_index in range(seq_count):
            final_state, outputs = run_chain(start_state, batches, inner_gain[layer_index])
            if round_index < seq_count - 1:
                start_state = jax.tree.map(
                    lambda own_init, incoming: jnp.where(seq_place == 0, own_init, incoming),
                    initial,
                    hand_over(final_state),
                )
        mixed = outputs.astype(jnp.bfloat16)
        projection = out_weight[layer_index]
        summed = lax.psum_scatter(
            jnp.dot(mixed, projection, preferred_element_type=jnp.float32).astype(jnp.bfloat16),
            "head",
            scatter_dimension=0,
            tiled=True,
        ).astype(jnp.float32)
        stream = (stream.astype(jnp.float32) + summed).astype(jnp.bfloat16)
    return stream


def solution(mesh):
    in_specs = (
        P(("dp", "seq", "head"), None),
        P(),
        P(None, None, "head"),
        P(None, None, "head"),
        P(None, "head"),
        P(None, "head", None, None),
        P(None, "head", None, None),
        P(None, "head", None),
        P(None, "head", None),
    )
    out_specs = P(("dp", "seq", "head"), None)
    return jax.shard_map(body, mesh=mesh, in_specs=in_specs, out_specs=out_specs, check_vma=False)
```

profile of v0, /device:TPU:24, one launch (start us, length us, event | category | flops | bytes accessed | tf_op | source)
XLA Modules:
  0.0 1143.0 jit_solution(8710354500398700739)
XLA Ops:
  7.3 10.1 slice_bitcast_fusion
  17.4 10.4 copy.68
  30.5 44.5 %all-gather.3.cloned.1.call-done = bf16[512,3072]{1,0:T(8,128)(2,1)} async-done(((bf16[64,3072]{1,0:T(8,128)(2,1)}), bf16[512,3072]{1,0:T(8,128)(2,1)}) %all-gather.3.cloned.1.call-update) | async-done | bytes 3145744 | tf_op jit(solution)/shard_map/all_gather | solution.py:81
  74.9 2.7 fusion.484
  79.0 10.6 convolution_bitcast_fusion.1
  92.8 79.8 %while.116 = (s32[]{:T(128)}, f32[6,64,256]{2,1,0:T(8,128)}, f32[6,64,256]{2,1,0:T(8,128)}, f32[8,6,64,64]{3,2,1,0:T(8,128)S(1)}, f32[8,6,64]{2,1,0:T(8,128)}, /...) while((s32[]{:T(128)}, f32[6,64,256]{2,1,0:T(8,128)}, f32[6,64,256]{2,1,0:T(8,128)}, ...), condition=%wide.region_6.7_spmd, body=%wide.region_1.6_spmd.sunk | while | flops 68447232 | bytes 8994465 | solution.py:74
  97.9 2.7 fusion.645
  107.9 2.7 fusion.645
  117.8 2.7 fusion.645
  127.8 2.7 fusion.645
  137.8 2.7 fusion.645
  147.8 2.7 fusion.645
  157.7 2.7 fusion.645
  167.7 2.7 fusion.645
  178.0 6.0 collective-permute-done.1
  187.6 80.0 %while.117 = (s32[]{:T(128)}, f32[6,64,256]{2,1,0:T(8,128)}, f32[6,64,256]{2,1,0:T(8,128)}, f32[8,6,64,64]{3,2,1,0:T(8,128)S(1)}, f32[8,6,64]{2,1,0:T(8,128)}, /...) while((s32[]{:T(128)}, f32[6,64,256]{2,1,0:T(8,128)}, f32[6,64,256]{2,1,0:T(8,128)}, ...), condition=%wide.region_12.13_spmd, body=%wide.region_7.12_spmd.sunk | while | flops 68447232 | bytes 8994465 | solution.py:74
  192.7 2.7 fusion.657
  202.7 2.7 fusion.657
  212.7 2.7 fusion.657
  222.7 2.7 fusion.657
  232.7 2.7 fusion.657
  242.7 2.7 fusion.657
  252.7 2.7 fusion.657
  262.7 2.7 fusion.657
  273.2 5.4 collective-permute-done.3
  282.1 80.0 %while.118 = (s32[]{:T(128)}, f32[6,64,256]{2,1,0:T(8,128)}, f32[6,64,256]{2,1,0:T(8,128)}, f32[8,6,64,64]{3,2,1,0:T(8,128)S(1)}, f32[8,6,64]{2,1,0:T(8,128)}, /...) while((s32[]{:T(128)}, f32[6,64,256]{2,1,0:T(8,128)}, f32[6,64,256]{2,1,0:T(8,128)}, ...), condition=%wide.region_18.19_spmd, body=%wide.region_13.18_spmd.sunk | while | flops 68447232 | bytes 8994465 | solution.py:74
  287.2 2.7 fusion.669
  297.2 2.7 fusion.669
  307.2 2.7 fusion.669
  317.2 2.7 fusion.669
  327.2 2.7 fusion.669
  347.2 2.7 fusion.669
  357.3 2.7 fusion.669
  367.5 5.8 collective-permute-done.5
  377.8 109.9 %while.119 = (s32[]{:T(128)}, f32[6,64,256]{2,1,0:T(8,128)}, f32[6,64,256]{2,1,0:T(8,128)}, bf16[8,6,64,64]{3,2,1,0:T(8,128)(2,1)}, f32[8,6,64,64]{3,2,1,0:T(8,1...) while((s32[]{:T(128)}, f32[6,64,256]{2,1,0:T(8,128)}, ...), condition=%wide.region_26.27_spmd, body=%wide.region_19.26_spmd.sunk | while | flops 94891392 | bytes 10780337 | solution.py:74
  382.9 2.7 fusion.682
  396.6 2.7 fusion.682
  410.4 2.7 fusion.682
  424.1 2.7 fusion.682
  437.8 2.7 fusion.682
  451.6 2.7 fusion.682
  489.7 5.2 convolution_convert_fusion.25
  495.0 77.8 %reduce-scatter.3.cloned.1.call-done = bf16[64,3072]{1,0:T(8,128)(2,1)} async-done(((bf16[512,3072]{1,0:T(8,128)(2,1)}), bf16[64,3072]{1,0:T(8,128)(2,1)}) %reduce-scatter.3.cloned.1.call-update) | async-done | bytes 393232 | tf_op jit(solution)/shard_map/reduce_scatter | solution.py:124
  574.9 10.3 copy.73
  585.2 51.9 %all-gather.5.cloned.1.call-done = bf16[512,3072]{1,0:T(8,128)(2,1)} async-done(((bf16[64,3072]{1,0:T(8,128)(2,1)}), bf16[512,3072]{1,0:T(8,128)(2,1)}) %all-gather.5.cloned.1.call-update) | async-done | bytes 3145744 | tf_op jit(solution)/shard_map/all_gather | solution.py:81
  637.1 2.7 fusion.487
  641.1 10.6 convolution_bitcast_fusion
  654.9 80.0 %while.120 = (s32[]{:T(128)}, f32[6,64,256]{2,1,0:T(8,128)}, f32[6,64,256]{2,1,0:T(8,128)}, f32[8,6,64,64]{3,2,1,0:T(8,128)S(1)}, f32[8,6,64]{2,1,0:T(8,128)}, /...) while((s32[]{:T(128)}, f32[6,64,256]{2,1,0:T(8,128)}, f32[6,64,256]{2,1,0:T(8,128)}, ...), condition=%wide.region_34.35_spmd, body=%wide.region_29.34_spmd.sunk | while | flops 68447232 | bytes 8994465 | solution.py:74
  660.0 2.7 fusion.695
  670.0 2.7 fusion.695
  680.0 2.7 fusion.695
  690.0 2.7 fusion.695
  700.0 2.7 fusion.695
  710.0 2.7 fusion.695
  720.0 2.7 fusion.695
  730.0 2.7 fusion.695
  740.3 6.0 collective-permute-done.7
  749.9 80.0 %while.121 = (s32[]{:T(128)}, f32[6,64,256]{2,1,0:T(8,128)}, f32[6,64,256]{2,1,0:T(8,128)}, f32[8,6,64,64]{3,2,1,0:T(8,128)S(1)}, f32[8,6,64]{2,1,0:T(8,128)}, /...) while((s32[]{:T(128)}, f32[6,64,256]{2,1,0:T(8,128)}, f32[6,64,256]{2,1,0:T(8,128)}, ...), condition=%wide.region_40.41_spmd, body=%wide.region_35.0_spmd.sunk | while | flops 68447232 | bytes 8994465 | solution.py:74
  835.5 5.4 collective-permute-done.9
  844.3 80.0 %while.122 = (s32[]{:T(128)}, f32[6,64,256]{2,1,0:T(8,128)}, f32[6,64,256]{2,1,0:T(8,128)}, f32[8,6,64,64]{3,2,1,0:T(8,128)S(1)}, f32[8,6,64]{2,1,0:T(8,128)}, /...) while((s32[]{:T(128)}, f32[6,64,256]{2,1,0:T(8,128)}, f32[6,64,256]{2,1,0:T(8,128)}, ...), condition=%wide.region_46.47_spmd, body=%wide.region_41.46_spmd.sunk | while | flops 68447232 | bytes 8994465 | solution.py:74
  929.0 5.6 collective-permute-done.11
  939.0 109.8 %while.123 = (s32[]{:T(128)}, f32[6,64,256]{2,1,0:T(8,128)}, f32[6,64,256]{2,1,0:T(8,128)}, bf16[8,6,64,64]{3,2,1,0:T(8,128)(2,1)}, f32[8,6,64,64]{3,2,1,0:T(8,1...) while((s32[]{:T(128)}, f32[6,64,256]{2,1,0:T(8,128)}, ...), condition=%wide.region_54.55_spmd, body=%wide.region_47.54_spmd.sunk | while | flops 94891392 | bytes 10780337 | solution.py:74
  1050.9 5.2 convolution_convert_fusion.24
  1056.0 78.2 %reduce-scatter.5.cloned.1.call-done = bf16[64,3072]{1,0:T(8,128)(2,1)} async-done(((bf16[512,3072]{1,0:T(8,128)(2,1)}), bf16[64,3072]{1,0:T(8,128)(2,1)}) %reduce-scatter.5.cloned.1.call-update) | async-done | bytes 393232 | tf_op jit(solution)/shard_map/reduce_scatter | solution.py:124
  (1196 shorter events, 671.7 us)
Async XLA Ops:
  6.5 68.4 %all-gather.3.cloned.1.call-start = ((), (), s32[]{:S(2)}) async-start(), calls=%async_computation.2 | async-start | bytes 3538944 | tf_op jit(solution)/shard_map/all_gather | solution.py:81
  7.3 565.5 %reduce-scatter.3.cloned.1.call-start = ((), (), s32[]{:S(2)}) async-start(), calls=%async_computation.3 | async-start | bytes 3538944 | tf_op jit(solution)/shard_map/reduce_scatter | solution.py:124
  17.4 10.4 copy-start.32
  17.4 10.5 copy-start.33
  17.4 10.5 copy-start.16
  17.4 10.5 copy-start.17
  74.9 2.8 copy-start.24
  97.9 2.7 copy-start.1
  107.9 2.7 copy-start.1
  117.8 2.7 copy-start.1
  127.8 2.7 copy-start.1
  137.8 2.7 copy-start.1
  147.8 2.7 copy-start.1
  167.7 2.7 copy-start.1
  174.2 9.7 collective-permute-start.1
  175.5 11.2 copy-start.18
  176.7 10.1 collective-permute-start
  202.7 2.7 copy-start.3
  222.7 2.7 copy-start.3
  232.7 2.7 copy-start.3
  242.7 2.7 copy-start.3
  252.7 2.7 copy-start.3
  262.7 2.7 copy-start.3
  269.3 9.3 collective-permute-start.3
  270.6 10.7 copy-start.19
  271.7 9.6 collective-permute-start.2
  287.2 2.7 copy-start.5
  307.2 2.7 copy-start.5
  317.2 2.7 copy-start.5
  327.2 2.7 copy-start.5
  347.2 2.7 copy-start.5
  357.3 2.7 copy-start.5
  363.8 9.5 collective-permute-start.5
  365.1 10.7 copy-start.20
  366.2 9.6 collective-permute-start.4
  382.9 2.7 copy-start.7
  396.6 2.7 copy-start.7
  410.4 2.7 copy-start.7
  424.1 2.7 copy-start.7
  437.8 2.7 copy-start.7
  451.6 2.7 copy-start.7
  494.9 77.9 %copy-start.27 = (bf16[64,3072]{1,0:T(8,128)(2,1)S(1)}, bf16[64,3072]{1,0:T(8,128)(2,1)}, u32[]{:S(2)}) copy-start(bf16[64,3072]{1,0:T(8,128)(2,1)} %param.25) | copy-start | bytes 1179652
  494.9 142.2 %all-gather.5.cloned.1.call-start = ((), (), s32[]{:S(2)}) async-start(), calls=%async_computation.4 | async-start | bytes 3538944 | tf_op jit(solution)/shard_map/all_gather | solution.py:81
  574.6 559.6 %reduce-scatter.5.cloned.1.call-start = ((), (), s32[]{:S(2)}) async-start(), calls=%async_computation.5 | async-start | bytes 3538944 | tf_op jit(solution)/shard_map/reduce_scatter | solution.py:124
  585.2 54.6 %copy-start.30 = (f32[1,3072]{1,0:T(1,128)S(1)}, f32[1,3072]{1,0:T(1,128)}, u32[]{:S(2)}) copy-start(f32[1,3072]{1,0:T(1,128)} %get-tuple-element.979) | copy-start | bytes 36868
  637.1 2.8 copy-start.25
  660.0 2.7 copy-start.9
  670.0 2.7 copy-start.9
  680.0 2.7 copy-start.9
  690.0 2.7 copy-start.9
  700.0 2.7 copy-start.9
  710.0 2.7 copy-start.9
  720.0 2.7 copy-start.9
  730.0 2.7 copy-start.9
  736.6 9.7 collective-permute-start.7
  737.9 11.3 copy-start.21
  739.0 10.2 collective-permute-start.6
  831.5 9.3 collective-permute-start.9
  832.8 10.7 copy-start.22
  833.9 9.6 collective-permute-start.8
  924.3 12.9 %copy-start.23 = (f32[2,6,64,256]{3,2,1,0:T(8,128)S(1)}, f32[2,6,64,256]{3,2,1,0:T(8,128)}, u32[]{:S(2)}) copy-start(f32[2,6,64,256]{3,2,1,0:T(8,128)} %param.30) | copy-start | bytes 2359300
  925.4 9.2 collective-permute-start.11
  927.7 9.5 collective-permute-start.10
  1056.0 78.2 %copy-start.26 = (bf16[64,3072]{1,0:T(8,128)(2,1)S(1)}, bf16[64,3072]{1,0:T(8,128)(2,1)}, u32[]{:S(2)}) copy-start(bf16[64,3072]{1,0:T(8,128)(2,1)} %add_convert_fusion.1) | copy-start | bytes 1179652
  (98 other events, 179.6 us)
Sparse Core Ops, SparseCore 0:
  9.7 65.2 all-gather.2
  495.0 77.6 reduce-scatter.2
  575.4 61.6 all-gather.4
  1056.2 78.0 reduce-scatter.4
where the time goes:
time: 1160 us; the launch traced here: 1140 us
  matrix products  537 us (46%)
  waiting for transfers between devices  293 us (25%)
  other arithmetic  224 us (19%)
  local copies, waits for them, and re-layouts  53.8 us (5%)
  starting transfers between devices  16.2 us (1%)
  between operations  13.9 us (1%)
    dot_general x272, matrix products, narrow_product(): jnp.einsum(form, left.astype(jnp.bfloat16), right.astype(jnp.bfloat16), p...  504 us
    reduce_scatter x2, waiting for transfers between devices, body(): lax.psum_scatter(jnp.dot(mixed, projection, preferred_element_type=jnp.fl...  156 us
    all_gather x2, waiting for transfers between devices, widen(): return lax.all_gather(stream, 'head', axis=0, tiled=True)  96.4 us
    reduce_sum x64, other arithmetic, inner_apply(): centre = result - jnp.mean(result, axis=-1, keepdims=True)  64.6 us
    mul x64, other arithmetic, inner_loss(): gate_rates[..., None] * differ * differ  44.1 us
    ppermute x12, waiting for transfers between devices, from_behind(): return lax.ppermute(block, axis, route)  39.4 us
    dot_general x3, local copies, waits for them, and re-layouts, project_inputs(): packed = jnp.dot(normed, qkv_cols, preferred_element_type=jnp.float32)  30.8 us
    dynamic_update_slice x16, other arithmetic, run_chain(): lax.scan(partial(update, gain_rows), start_state, batches)  27.8 us
  transfers between devices with their start and end apart: 16, of which 16 were waited for; matrix products, arithmetic and copies ran while one was open for 4% of the time, Pallas kernels for 0%

commit v1 on v0

v1 whole, which is shorter than its diff:
```python
import functools

import jax
import jax.numpy as jnp
from jax import lax
from jax.experimental import pallas as pl
from jax.experimental.pallas import tpu as pltpu
from jax.sharding import PartitionSpec as P

F32 = jnp.float32
B16 = jnp.bfloat16
MB = 64
GELU_A = 0.7978845608028654
GELU_B = 0.044715
NN = (((1,), (0,)), ((), ()))
NT = (((1,), (1,)), ((), ()))


def dot(left, right, dims=NN):
    return lax.dot_general(left, right, dims, preferred_element_type=F32)


def first_half(shape):
    return lax.broadcasted_iota(jnp.int32, shape, len(shape) - 1) < 64


def spread(x):
    mask = first_half(x.shape)
    zero = jnp.zeros_like(x)
    return jnp.concatenate([jnp.where(mask, x, zero), jnp.where(mask, zero, x)], axis=0)


def flip(x):
    y = spread(x).T
    return y[:64] + y[64:]


def fold(y):
    return jnp.where(first_half((64, 128)), y[:64], y[64:])


def mean0(x):
    return jnp.sum(x, axis=0, keepdims=True) * (1.0 / 64)


def normalise(y):
    centre = y - mean0(y)
    scale = lax.rsqrt(mean0(centre * centre) + 1e-5)
    return centre * scale, scale


def gelu_parts(h):
    square = h * h
    t = jnp.tanh(h * (GELU_A + (GELU_A * GELU_B) * square))
    half = 0.5 * h
    return square, t, half, half + half * t


def chain_steps(pairs, batches, qkv, rate, gain, w1, w2, out, rows, target):
    def block(b):
        return pl.ds(pl.multiple_of(b * MB, MB), MB)

    def tiles(b, p):
        return [qkv[block(b), p * 384 + j * 128 : p * 384 + (j + 1) * 128] for j in range(3)]

    def queries(b, p):
        t0, t1, _ = tiles(b, p)
        return jnp.where(first_half(t0.shape), t0, t1)

    def prepare_keys(b):
        for p in range(pairs):
            t0, t1, t2 = tiles(b, p)
            mask = first_half(t0.shape)
            keys = pltpu.roll(jnp.where(mask, t2, t0), 64, 1)
            values = jnp.where(mask, t1, t2)
            rows[p, 0:128] = spread(keys).astype(B16)
            target[p] = flip(values - keys)

    def prepare_queries(b):
        for p in range(pairs):
            rows[p, 128:256] = spread(queries(b, p)).astype(B16)

    def put(b, p, y):
        result = queries(b, p) + flip(normalise(y)[0] * gain[p])
        out[block(b), p * 128 : (p + 1) * 128] = result.astype(B16)

    prepare_keys(0)
    rows[:, 128:256] = jnp.zeros((pairs, 128, 128), B16)

    def step(b, carry):
        first = [w1[p].astype(B16) for p in range(pairs)]
        second = [w2[p].astype(B16) for p in range(pairs)]
        hidden = [dot(first[p], rows[p], NT) for p in range(pairs)]
        act, slope, act_q = [], [], []
        for p in range(pairs):
            square, t, half, a = gelu_parts(hidden[p][:, :128])
            slope.append(0.5 + 0.5 * t + half * (1.0 - t * t) * (GELU_A + (3 * GELU_A * GELU_B) * square))
            act.append(a.astype(B16))
        for p in range(pairs):
            act_q.append(gelu_parts(hidden[p][:, 128:])[3].astype(B16))
        result, result_q = [], []
        for p in range(pairs):
            turned = second[p].T
            result.append(fold(dot(turned, act[p])))
            result_q.append(fold(dot(turned, act_q[p])))
        cotangent = []
        for p in range(pairs):
            y, scale = normalise(result[p])
            dy = (y * gain[p] - target[p]) * rate[b, p] * gain[p]
            dy = scale * (dy - mean0(dy) - y * mean0(dy * y))
            cotangent.append(spread(dy).astype(B16))
        for p in range(pairs):
            down = (dot(second[p], cotangent[p]) * slope[p]).astype(B16)
            w1[p] = w1[p] - dot(down, rows[p, 0:128])
            w2[p] = w2[p] - dot(act[p], cotangent[p], NT)
        for p in range(pairs):
            put(jnp.maximum(b - 1, 0), p, result_q[p])
        prepare_keys(jnp.minimum(b + 1, batches - 1))
        prepare_queries(b)
        return carry

    lax.fori_loop(0, batches, step, 0)
    for p in range(pairs):
        hidden = dot(w1[p].astype(B16), rows[p, 128:256], NT)
        a = gelu_parts(hidden)[3].astype(B16)
        put(batches - 1, p, fold(dot(w2[p].astype(B16).T, a)))


def chain_kernel(pairs, batches, turn, *refs):
    active, qkv, rate, gain, state = refs[:5]
    out, state_out = refs[-13:-11] if turn == 0 else refs[-12:-10]
    scratch = refs[-11:] if turn == 0 else refs[-10:]
    qkv_v, rate_v, gain_v, state_v, out_v, w1, w2, rows, target, sems = scratch[-10:]
    final = scratch[0] if turn == 0 else state_v

    @pl.when(active[0] == turn)
    def _():
        moves = [
            pltpu.make_async_copy(a, b, sems.at[i])
            for i, (a, b) in enumerate([(qkv, qkv_v), (rate, rate_v), (gain, gain_v), (state, state_v)])
        ]
        for move in moves:
            move.start()
        for move in moves:
            move.wait()
        w1[...] = state_v[0].astype(F32)
        w2[...] = state_v[1].astype(F32)
        chain_steps(pairs, batches, qkv_v, rate_v, gain_v, w1, w2, out_v, rows, target)
        final[0] = w1[...].astype(B16)
        final[1] = w2[...].astype(B16)
        back = [
            pltpu.make_async_copy(final, state_out, sems.at[0]),
            pltpu.make_async_copy(out_v, out, sems.at[1]),
        ]
        for move in back:
            move.start()
        for move in back:
            move.wait()


def run_chain(turn, place, qkv, rate, gain, state, out):
    tokens = qkv.shape[0]
    pairs = state.shape[1]
    batches = tokens // MB
    first = turn == 0
    anywhere = pl.BlockSpec(memory_space=pl.ANY)
    scratch = [
        pltpu.VMEM(qkv.shape, F32),
        pltpu.VMEM(rate.shape, F32),
        pltpu.VMEM(gain.shape, F32),
        pltpu.VMEM(state.shape, state.dtype),
        pltpu.VMEM((tokens, pairs * 128), B16),
        pltpu.VMEM(state.shape[1:], F32),
        pltpu.VMEM(state.shape[1:], F32),
        pltpu.VMEM((pairs, 256, 128), B16),
        pltpu.VMEM((pairs, 64, 128), F32),
        pltpu.SemaphoreType.DMA((4,)),
    ]
    if first:
        scratch = [pltpu.VMEM(state.shape, B16)] + scratch
    operands = [place, qkv, rate, gain, state] + ([] if first else [out])
    return pl.pallas_call(
        functools.partial(chain_kernel, pairs, batches, turn),
        out_shape=[
            jax.ShapeDtypeStruct((tokens, pairs * 128), B16),
            jax.ShapeDtypeStruct(state.shape, B16),
        ],
        in_specs=[pl.BlockSpec(memory_space=pltpu.SMEM)] + [anywhere] * (len(operands) - 1),
        out_specs=[anywhere, anywhere],
        scratch_shapes=scratch,
        input_output_aliases={} if first else {5: 0},
        compiler_params=pltpu.CompilerParams(vmem_limit_bytes=32 << 20),
        name=f"chain_{turn}",
    )(*operands)


def product_kernel(left, right, out):
    out[...] = dot(left[...], right[0]).astype(out.dtype)


def product(left, stack, layer, tile, kind):
    rows, depth = left.shape
    columns = stack.shape[2]
    return pl.pallas_call(
        product_kernel,
        grid=(columns // tile,),
        out_shape=jax.ShapeDtypeStruct((rows, columns), kind),
        in_specs=[
            pl.BlockSpec((rows, depth), lambda i: (0, 0)),
            pl.BlockSpec((1, depth, tile), lambda i: (layer, 0, i)),
        ],
        out_specs=pl.BlockSpec((rows, tile), lambda i: (0, i)),
        compiler_params=pltpu.CompilerParams(vmem_limit_bytes=32 << 20),
        name="product",
    )(left, stack)


def to_head_order(block):
    count = lax.axis_size("head")
    return lax.all_to_all(jnp.broadcast_to(block[None], (count,) + block.shape), "head", 0, 0, tiled=True)


def body(tokens, norm_gain, qkv_weight, rate_weight, rate_base, fast_first, fast_second, inner_gain, out_weight):
    seq_count = lax.axis_size("seq")
    place = lax.axis_index("seq").astype(jnp.int32).reshape(1)
    layers, heads = rate_base.shape
    pairs = heads // 2

    def turned(weights):
        return weights.reshape(layers, pairs, 128, 256).swapaxes(2, 3)

    initial = jnp.stack([turned(fast_first), turned(fast_second)], axis=1)
    gains = jnp.repeat(inner_gain.reshape(layers, pairs, 2, 64).swapaxes(2, 3), MB, axis=3)
    stream = tokens.astype(F32)
    for layer in range(layers):
        mean_square = jnp.mean(stream * stream, axis=-1, keepdims=True)
        normed = (stream * lax.rsqrt(mean_square + 1e-06) * norm_gain[layer]).astype(B16)
        rows = to_head_order(normed).reshape(-1, normed.shape[1])
        qkv = product(rows, qkv_weight, layer, 384, F32)
        batches = rows.shape[0] // MB
        rate = jax.nn.sigmoid(jnp.dot(rows, rate_weight[layer], preferred_element_type=F32))
        rate = rate * (rate_base[layer] * (1.0 / MB))
        rate = rate.reshape(batches, MB, pairs, 2).transpose(0, 2, 3, 1).reshape(batches, pairs, 1, 128)
        state, mixed = initial[layer], None
        for turn in range(seq_count):
            mixed, state = run_chain(turn, place, qkv, rate, gains[layer], state, mixed)
            if turn < seq_count - 1:
                state = lax.ppermute(state, "seq", [(turn, turn + 1)])
        parts = product(mixed, out_weight, layer, 1024, B16).reshape(lax.axis_size("head"), -1, stream.shape[1])
        parts = lax.all_to_all(parts, "head", 0, 0, tiled=True)
        summed = jnp.sum(parts.astype(F32), axis=0)
        out = (stream + summed).astype(B16)
        stream = out.astype(F32)
    return out


def solution(mesh):
    rows = P(("dp", "seq", "head"), None)
    in_specs = (
        rows,
        P(),
        P(None, None, "head"),
        P(None, None, "head"),
        P(None, "head"),
        P(None, "head", None, None),
        P(None, "head", None, None),
        P(None, "head", None),
        P(None, "head", None),
    )
    return jax.shard_map(body, mesh=mesh, in_specs=in_specs, out_specs=rows, check_vma=False)
```

time: 1160 us -> 329 us (0.28); the launches traced: 1140 us -> 328 us
  matrix products: 537 us -> 1.86 us
  other arithmetic: 224 us -> 7.22 us
  waiting for transfers between devices: 293 us -> 150 us
  blocking collectives: 0 us -> 80.3 us
  Pallas kernels: 0 us -> 40 us
  local copies, waits for them, and re-layouts: 53.8 us -> 31 us
  between operations: 13.9 us -> 0.38 us
    dot_general x278 -> x2, matrix products: 537 us -> 1.86 us  [body(): jnp.dot(rows, rate_weight[layer], preferred_element_type=F32)]
    reduce_scatter x2 -> x0, waiting for transfers between devices: 156 us -> none  [body(): lax.psum_scatter(jnp.dot(mixed, projection, preferred_element_type=jnp.fl...]
    reduce_sum x210 -> x4, other arithmetic: 114 us -> 2.43 us  [the longest x2 1.39 us: body(): mean_square = jnp.mean(stream * stream, axis=-1, keepdims=True)]
    all_gather x2 -> x0, waiting for transfers between devices: 96.4 us -> none  [widen(): return lax.all_gather(stream, 'head', axis=0, tiled=True)]
    all_to_all x0 -> x2, blocking collectives: none -> 80.3 us  [body(): parts = lax.all_to_all(parts, 'head', 0, 0, tiled=True)]
    all_to_all x0 -> x2, waiting for transfers between devices: none -> 77.9 us  [to_head_order(): lax.all_to_all(jnp.broadcast_to(block[None], (count,) + block.shape), 'he...]
    mul x64 -> x1, other arithmetic: 44.1 us -> 0.01 us  [body(): rate = rate * (rate_base[layer] * (1.0 / MB))]
    pallas_call x0 -> x12, Pallas kernels: none -> 40 us  [the longest x8 22.6 us: run_chain(): pl.pallas_call(functools.partial(chain_kernel, pairs, batches, turn), out...]
  transfers between devices with their start and end apart: 16 -> 8, of which waited for: 16 -> 4; matrix products, arithmetic and copies ran while one was open for 4% -> 3% of each run, Pallas kernels for 0% -> 0%
where the time goes in v1:
time: 329 us; the launch traced here: 328 us
  waiting for transfers between devices  150 us (46%)
  blocking collectives  80.3 us (24%)
  Pallas kernels  40 us (12%)
  local copies, waits for them, and re-layouts  31 us (9%)
  starting transfers between devices  16.7 us (5%)
  other arithmetic  7.22 us (2%)
    all_to_all x2, blocking collectives, body(): parts = lax.all_to_all(parts, 'head', 0, 0, tiled=True)  80.3 us
    all_to_all x2, waiting for transfers between devices, to_head_order(): lax.all_to_all(jnp.broadcast_to(block[None], (count,) + block.shape), 'he...  77.9 us
    ppermute x6, waiting for transfers between devices, body(): state = lax.ppermute(state, 'seq', [(turn, turn + 1)])  72.2 us
    pallas_call x8, Pallas kernels, run_chain(): pl.pallas_call(functools.partial(chain_kernel, pairs, batches, turn), out...  22.6 us
    unnamed x28, local copies, waits for them, and re-layouts  19.9 us
    pallas_call x4, Pallas kernels, product(): pl.pallas_call(product_kernel, grid=(columns // tile,), out_shape=jax.Sha...  17.4 us
    all_to_all x2, starting transfers between devices, to_head_order(): lax.all_to_all(jnp.broadcast_to(block[None], (count,) + block.shape), 'he...  11.4 us
  transfers between devices with their start and end apart: 8, of which 4 were waited for; matrix products, arithmetic and copies ran while one was open for 3% of the time, Pallas kernels for 0%

profile of v1, /device:TPU:24, one launch (start us, length us, event | category | flops | bytes accessed | tf_op | source)
XLA Modules:
  0.0 327.6 jit_solution(17178859125444835926)
XLA Ops:
  0.0 0.8 fusion.21
  0.8 1.2 fusion.8
  2.0 1.2 fusion.10
  3.2 2.0 broadcast_in_dim.12
  5.2 7.7 %all-to-all-start = ((bf16[8,64,3072]{2,1,0:T(8,128)(2,1)}), bf16[8,64,3072]{2,1,0:T(8,128)(2,1)S(1)}, u32[]{:S(2)}, u32[]{:S(2)}) async-start(bf16[8,64,3072]{2,1,0:T(8,128)(2,1)} %broadcast_in_dim.12), calls=%async_computation | async-start | bytes 6291456 | tf_op jit(solution)/shard_map/all_to_all | solution.py:220
  13.0 0.0 copy-done.12
  13.0 0.1 copy.22
  13.1 0.3 broadcast_in_dim.26
  13.4 0.2 broadcast_in_dim.27.refs_3_
  13.5 2.3 copy.23
  15.9 2.3 copy.24
  18.2 2.6 fusion.18
  20.8 0.0 copy-done.13
  20.8 0.1 fusion.20
  20.9 37.5 %all-to-all-done = bf16[8,64,3072]{2,1,0:T(8,128)(2,1)S(1)} async-done(((bf16[8,64,3072]{2,1,0:T(8,128)(2,1)}), bf16[8,64,3072]{2,1,0:T(8,128)(2,1)S(1)}, u32[]{:S(2)}, u32[]{:S(2)}) %all-to-all-start) | async-done | bytes 3145760 | tf_op jit(solution)/shard_map/all_to_all | solution.py:220
  58.4 0.9 fusion.7
  59.4 0.1 reshape.65
  59.4 0.1 reshape.66.refs_2_
  59.5 0.0 copy-start
  59.6 5.0 %copy-done = bf16[2,3072,1152]{2,1,0:T(8,128)(2,1)S(1)} copy-done((bf16[2,3072,1152]{2,1,0:T(8,128)(2,1)S(1)}, bf16[2,3072,1152]{2,1,0:T(8,128)(2,1)}, u32[]{:S(2)}) %copy-start) | copy-done | bytes 14155800
  64.6 6.2 %product.4.refs_1_ = f32[512,1152]{1,0:T(8,128)S(1)} custom-call(bf16[512,3072]{1,0:T(8,128)(2,1)S(1)} %bitcast.47, bf16[2,3072,1152]{2,1,0:T(8,128)(2,1)S(1)} %copy-done), custom_call_target="tpu_custom_call" | custom-call | tf_op jit(solution)/shard_map/product/pallas_call | solution.py:204
  70.9 0.7 collective-permute-start
  71.6 0.0 collective-permute-done.refs_4_
  71.6 0.7 collective-permute-start.1
  72.3 0.0 collective-permute-done.1.refs_4_
  72.4 1.3 collective-permute-start.2
  73.7 57.5 %collective-permute-done.2.refs_4_ = bf16[2,3,256,128]{3,2,1,0:T(8,128)(2,1)S(1)} collective-permute-done((bf16[2,3,256,128]{3,2,1,0:T(8,128)(2,1)S(1)}, bf16[2,3,256,128]{3,2,1,0:T(8,128)(2,1)S(1)}, u32[]{:S(2)}, u32[]{:S(2)}) %collective-permute-start.2) | collective-permute-done | bytes 393248 | tf_op jit(solution)/shard_map/ppermute | solution.py:248
  131.2 11.2 %chain_3.2 = (bf16[512,384]{1,0:T(8,128)(2,1)S(1)}, bf16[2,3,256,128]{3,2,1,0:T(8,128)(2,1)}) custom-call(s32[1]{0:T(128)} %bitcast.refs_0_, f32[512,1152]{1,0:T(8,128)S(1)} %product.4.refs_1_, f32[8,3,1,128]{3,2,1,0:T(1,128)S(1)} %reshape.66.refs_2_, f32[3,64,128]{2,1,0:T(8,128)S(1)} %broadcast_in_dim.27.refs_3_, ...), custom_call_target="tpu_custom_call", output_to_operand_aliasing={{0}: (5, {})} | custom-call | tf_op jit(solution)/shard_map/chain_3/pallas_call | solution.py:182
  142.4 0.0 copy-start.4
  142.4 2.3 copy-done.4
  144.7 2.5 product.5
  147.2 42.6 %all_to_all.20 = bf16[8,64,3072]{2,1,0:T(8,128)(2,1)S(1)} all-to-all(bf16[8,64,3072]{2,1,0:T(8,128)(2,1)S(1)} %bitcast.50), channel_id=1, replica_groups=mesh['seq'=4,'head'=8,'dp'=4] {'head'}, dimensions={0} | all-to-all | bytes 6291456 | tf_op jit(solution)/shard_map/all_to_all | solution.py:250
  189.8 0.5 convert_reduce_fusion.1
  190.3 0.5 copy-done.8
  190.8 0.2 fusion.12
  191.0 0.7 copy-done.9
  191.8 0.2 fusion.14
  191.9 2.0 broadcast_in_dim.28
  193.9 3.6 %all-to-all-start.2 = ((bf16[8,64,3072]{2,1,0:T(8,128)(2,1)}), bf16[8,64,3072]{2,1,0:T(8,128)(2,1)S(1)}, u32[]{:S(2)}, u32[]{:S(2)}) async-start(bf16[8,64,3072]{2,1,0:T(8,128)(2,1)} %broadcast_in_dim.28), calls=%async_computation.2 | async-start | bytes 6291456 | tf_op jit(solution)/shard_map/all_to_all | solution.py:220
  197.6 0.1 copy.27
  197.7 0.3 broadcast_in_dim.29
  198.0 0.2 broadcast_in_dim.30.refs_3_
  198.1 40.4 %all-to-all-done.2 = bf16[8,64,3072]{2,1,0:T(8,128)(2,1)S(1)} async-done(((bf16[8,64,3072]{2,1,0:T(8,128)(2,1)}), bf16[8,64,3072]{2,1,0:T(8,128)(2,1)S(1)}, u32[]{:S(2)}, u32[]{:S(2)}) %all-to-all-start.2) | async-done | bytes 3145760 | tf_op jit(solution)/shard_map/all_to_all | solution.py:220
  238.6 1.6 copy-done.2
  240.2 5.0 %copy-done.1 = bf16[2,3072,1152]{2,1,0:T(8,128)(2,1)S(1)} copy-done((bf16[2,3072,1152]{2,1,0:T(8,128)(2,1)S(1)}, bf16[2,3072,1152]{2,1,0:T(8,128)(2,1)}, u32[]{:S(2)}) %copy-start.1) | copy-done | bytes 14155800
  245.2 1.9 copy-done.3
  247.1 6.2 %product.6.refs_1_ = f32[512,1152]{1,0:T(8,128)S(1)} custom-call(bf16[512,3072]{1,0:T(8,128)(2,1)S(1)} %bitcast.48, bf16[2,3072,1152]{2,1,0:T(8,128)(2,1)S(1)} %copy-done.1), custom_call_target="tpu_custom_call" | custom-call | tf_op jit(solution)/shard_map/product/pallas_call | solution.py:204
  253.4 0.9 fusion.3
  254.3 0.1 reshape.72
  254.4 0.1 reshape.73.refs_2_
  254.6 0.7 collective-permute-start.3
  255.3 0.0 collective-permute-done.3.refs_4_
  255.3 0.7 collective-permute-start.4
  256.0 0.0 collective-permute-done.4.refs_4_
  256.1 1.3 collective-permute-start.5
  257.4 14.7 %collective-permute-done.5.refs_4_ = bf16[2,3,256,128]{3,2,1,0:T(8,128)(2,1)S(1)} collective-permute-done((bf16[2,3,256,128]{3,2,1,0:T(8,128)(2,1)S(1)}, bf16[2,3,256,128]{3,2,1,0:T(8,128)(2,1)S(1)}, u32[]{:S(2)}, u32[]{:S(2)}) %collective-permute-start.5) | collective-permute-done | bytes 393248 | tf_op jit(solution)/shard_map/ppermute | solution.py:248
  272.1 11.2 %chain_3.3 = (bf16[512,384]{1,0:T(8,128)(2,1)S(1)}, bf16[2,3,256,128]{3,2,1,0:T(8,128)(2,1)}) custom-call(s32[1]{0:T(128)} %bitcast.refs_0_, f32[512,1152]{1,0:T(8,128)S(1)} %product.6.refs_1_, f32[8,3,1,128]{3,2,1,0:T(1,128)S(1)} %reshape.73.refs_2_, f32[3,64,128]{2,1,0:T(8,128)S(1)} %broadcast_in_dim.30.refs_3_, ...), custom_call_target="tpu_custom_call", output_to_operand_aliasing={{0}: (5, {})} | custom-call | tf_op jit(solution)/shard_map/chain_3/pallas_call | solution.py:182
  283.3 0.0 copy-start.5
  283.3 2.3 copy-done.5
  285.6 2.5 product.7
  288.1 37.7 %all_to_all.21 = bf16[8,64,3072]{2,1,0:T(8,128)(2,1)S(1)} all-to-all(bf16[8,64,3072]{2,1,0:T(8,128)(2,1)S(1)} %bitcast.51), channel_id=1, replica_groups=mesh['seq'=4,'head'=8,'dp'=4] {'head'}, dimensions={0} | all-to-all | bytes 6291456 | tf_op jit(solution)/shard_map/all_to_all | solution.py:250
  325.8 0.5 convert_reduce_fusion
  326.3 0.5 copy-done.10
  326.8 0.8 fusion.15
  (26 shorter events, 0.3 us)
Async XLA Ops:
  5.2 7.7 %copy-start.12 = (f32[2,6,64]{2,0,1:T(2,128)S(1)}, f32[2,6,64]{2,0,1:T(2,128)}, u32[]{:S(2)}) copy-start(f32[2,6,64]{2,0,1:T(2,128)} %param.16) | copy-start | bytes 9220
  5.2 53.2 %all-to-all-start = ((bf16[8,64,3072]{2,1,0:T(8,128)(2,1)}), bf16[8,64,3072]{2,1,0:T(8,128)(2,1)S(1)}, u32[]{:S(2)}, u32[]{:S(2)}) async-start(bf16[8,64,3072]{2,1,0:T(8,128)(2,1)} %broadcast_in_dim.12), calls=%async_computation | async-start | bytes 6291456 | tf_op jit(solution)/shard_map/all_to_all | solution.py:220
  13.5 7.3 %copy-start.13 = (f32[2,6]{1,0:T(2,128)S(1)}, f32[2,6]{1,0:T(2,128)}, u32[]{:S(2)}) copy-start(f32[2,6]{1,0:T(2,128)} %param.13) | copy-start | bytes 148
  13.5 7.3 %copy-start.11 = (bf16[2,3072,6]{1,0,2:T(2,128)(2,1)S(1)}, bf16[2,3072,6]{1,0,2:T(2,128)(2,1)}, u32[]{:S(2)}) copy-start(bf16[2,3072,6]{1,0,2:T(2,128)(2,1)} %param.12) | copy-start | bytes 221188
  59.5 5.0 %copy-start = (bf16[2,3072,1152]{2,1,0:T(8,128)(2,1)S(1)}, bf16[2,3072,1152]{2,1,0:T(8,128)(2,1)}, u32[]{:S(2)}) copy-start(bf16[2,3072,1152]{2,1,0:T(8,128)(2,1)} %right.6) | copy-start | bytes 42467332
  64.6 6.2 %copy-start.7 = (f32[2,3,256,128]{3,2,1,0:T(8,128)S(1)}, f32[2,3,256,128]{3,2,1,0:T(8,128)}, u32[]{:S(2)}) copy-start(f32[2,3,256,128]{3,2,1,0:T(8,128)} %get-tuple-element.36.refs_4_) | copy-start | bytes 2359300
  70.9 0.7 collective-permute-start
  71.6 0.7 collective-permute-start.1
  72.4 58.8 %collective-permute-start.2 = (bf16[2,3,256,128]{3,2,1,0:T(8,128)(2,1)S(1)}, bf16[2,3,256,128]{3,2,1,0:T(8,128)(2,1)S(1)}, u32[]{:S(2)}, u32[]{:S(2)}) collective-permute-start(bf16[2,3,256,128]{3,2,1,0:T(8,128)(2,1)S(1)} %get-tuple-element.23), channel_id=1, source_target_pairs={{64,96},{65,97},{66,98},{67,99},{68,100},{69,101},{70,102},{71,103... | collective-permute-start | bytes 1179656 | tf_op jit(solution)/shard_map/ppermute | solution.py:248
  142.4 2.3 copy-start.4
  189.8 1.0 copy-start.8
  191.0 0.8 copy-start.9
  193.9 44.6 %all-to-all-start.2 = ((bf16[8,64,3072]{2,1,0:T(8,128)(2,1)}), bf16[8,64,3072]{2,1,0:T(8,128)(2,1)S(1)}, u32[]{:S(2)}, u32[]{:S(2)}) async-start(bf16[8,64,3072]{2,1,0:T(8,128)(2,1)} %broadcast_in_dim.28), calls=%async_computation.2 | async-start | bytes 6291456 | tf_op jit(solution)/shard_map/all_to_all | solution.py:220
  238.6 1.6 copy-start.2
  240.2 5.0 %copy-start.1 = (bf16[2,3072,1152]{2,1,0:T(8,128)(2,1)S(1)}, bf16[2,3072,1152]{2,1,0:T(8,128)(2,1)}, u32[]{:S(2)}) copy-start(bf16[2,3072,1152]{2,1,0:T(8,128)(2,1)} %right.6) | copy-start | bytes 42467332
  245.2 1.9 copy-start.3
  253.4 1.1 copy-start.6
  254.6 0.7 collective-permute-start.3
  255.3 0.7 collective-permute-start.4
  256.1 16.0 %collective-permute-start.5 = (bf16[2,3,256,128]{3,2,1,0:T(8,128)(2,1)S(1)}, bf16[2,3,256,128]{3,2,1,0:T(8,128)(2,1)S(1)}, u32[]{:S(2)}, u32[]{:S(2)}) collective-permute-start(bf16[2,3,256,128]{3,2,1,0:T(8,128)(2,1)S(1)} %get-tuple-element.30), channel_id=1, source_target_pairs={{64,96},{65,97},{66,98},{67,99},{68,100},{69,101},{70,102},{71,103... | collective-permute-start | bytes 1179656 | tf_op jit(solution)/shard_map/ppermute | solution.py:248
  283.3 2.3 copy-start.5
  325.8 1.0 copy-start.10

commit v2 on v1

v2 whole, which is shorter than its diff:
```python
import functools

import jax
import jax.numpy as jnp
from jax import lax
from jax.experimental import pallas as pl
from jax.experimental.pallas import tpu as pltpu
from jax.sharding import PartitionSpec as P

F32 = jnp.float32
B16 = jnp.bfloat16
MB = 64
GELU_A = 0.7978845608028654
GELU_B = 0.044715
NN = (((1,), (0,)), ((), ()))
NT = (((1,), (1,)), ((), ()))


def dot(left, right, dims=NN):
    return lax.dot_general(left, right, dims, preferred_element_type=F32)


def first_half(shape):
    return lax.broadcasted_iota(jnp.int32, shape, len(shape) - 1) < 64


def spread(x):
    mask = first_half(x.shape)
    zero = jnp.zeros_like(x)
    return jnp.concatenate([jnp.where(mask, x, zero), jnp.where(mask, zero, x)], axis=0)


def flip(x):
    y = spread(x).T
    return y[:64] + y[64:]


def fold(y):
    return jnp.where(first_half((64, 128)), y[:64], y[64:])


def mean0(x):
    return jnp.sum(x, axis=0, keepdims=True) * (1.0 / 64)


def normalise(y):
    centre = y - mean0(y)
    scale = lax.rsqrt(mean0(centre * centre) + 1e-5)
    return centre * scale, scale


def gelu_parts(h):
    square = h * h
    t = jnp.tanh(h * (GELU_A + (GELU_A * GELU_B) * square))
    half = 0.5 * h
    return square, t, half, half + half * t


def chain_steps(pairs, batches, where, qkv, rate, gain, w1, w2, out, rows, target):
    def block(b):
        return pl.ds(pl.multiple_of(where[b + 1] * MB, MB), MB)

    def rates(b, p):
        slot = rate[where[b + 1]]
        return jnp.concatenate([slot[2 * p : 2 * p + 1], slot[2 * p + 1 : 2 * p + 2]], axis=1)

    def tiles(b, p):
        return [qkv[block(b), p * 384 + j * 128 : p * 384 + (j + 1) * 128] for j in range(3)]

    def queries(b, p):
        t0, t1, _ = tiles(b, p)
        return jnp.where(first_half(t0.shape), t0, t1)

    def prepare_keys(b):
        for p in range(pairs):
            t0, t1, t2 = tiles(b, p)
            mask = first_half(t0.shape)
            keys = pltpu.roll(jnp.where(mask, t2, t0), 64, 1)
            values = jnp.where(mask, t1, t2)
            rows[p, 0:128] = spread(keys).astype(B16)
            target[p] = flip(values - keys)

    def prepare_queries(b):
        for p in range(pairs):
            rows[p, 128:256] = spread(queries(b, p)).astype(B16)

    def put(b, p, y):
        result = queries(b, p) + flip(normalise(y)[0] * gain[p])
        out[block(b), p * 128 : (p + 1) * 128] = result.astype(B16)

    prepare_keys(0)
    rows[:, 128:256] = jnp.zeros((pairs, 128, 128), B16)

    def step(b, carry):
        first = [w1[p].astype(B16) for p in range(pairs)]
        second = [w2[p].astype(B16) for p in range(pairs)]
        hidden = [dot(first[p], rows[p], NT) for p in range(pairs)]
        act, slope, act_q = [], [], []
        for p in range(pairs):
            square, t, half, a = gelu_parts(hidden[p][:, :128])
            slope.append(0.5 + 0.5 * t + half * (1.0 - t * t) * (GELU_A + (3 * GELU_A * GELU_B) * square))
            act.append(a.astype(B16))
        for p in range(pairs):
            act_q.append(gelu_parts(hidden[p][:, 128:])[3].astype(B16))
        result, result_q = [], []
        for p in range(pairs):
            turned = second[p].T
            result.append(fold(dot(turned, act[p])))
            result_q.append(fold(dot(turned, act_q[p])))
        cotangent = []
        for p in range(pairs):
            y, scale = normalise(result[p])
            dy = (y * gain[p] - target[p]) * rates(b, p) * gain[p]
            dy = scale * (dy - mean0(dy) - y * mean0(dy * y))
            cotangent.append(spread(dy).astype(B16))
        for p in range(pairs):
            down = (dot(second[p], cotangent[p]) * slope[p]).astype(B16)
            w1[p] = w1[p] - dot(down, rows[p, 0:128])
            w2[p] = w2[p] - dot(act[p], cotangent[p], NT)
        for p in range(pairs):
            put(jnp.maximum(b - 1, 0), p, result_q[p])
        prepare_keys(jnp.minimum(b + 1, batches - 1))
        prepare_queries(b)
        return carry

    lax.fori_loop(0, batches, step, 0)
    for p in range(pairs):
        hidden = dot(w1[p].astype(B16), rows[p, 128:256], NT)
        a = gelu_parts(hidden)[3].astype(B16)
        put(batches - 1, p, fold(dot(w2[p].astype(B16).T, a)))


def chain_kernel(pairs, first_pair, batches, turn, where, qkv_a, qkv_b, rate_a, rate_b, gain, state, *refs):
    out, state_out, qkv_v, rate_v, gain_v, state_v, final, out_v, w1, w2, rows, target, sems = refs[-13:]
    columns = pl.ds(first_pair * 384, pairs * 384)
    near, far = qkv_a.shape[0], qkv_b.shape[0]

    @pl.when(where[0] == turn)
    def _():
        moves = [
            (qkv_a.at[:, columns], qkv_v.at[pl.ds(0, near)]),
            (qkv_b.at[:, columns], qkv_v.at[pl.ds(near, far)]),
            (rate_a, rate_v.at[pl.ds(0, near // MB)]),
            (rate_b, rate_v.at[pl.ds(near // MB, far // MB)]),
            (gain.at[pl.ds(first_pair, pairs)], gain_v),
            (state, state_v),
        ]
        moves = [pltpu.make_async_copy(a, b, sems.at[i]) for i, (a, b) in enumerate(moves)]
        for move in moves:
            move.start()
        for move in moves:
            move.wait()
        w1[...] = state_v[0].astype(F32)
        w2[...] = state_v[1].astype(F32)
        chain_steps(pairs, batches, where, qkv_v, rate_v.at[:, pl.ds(2 * first_pair, 2 * pairs)], gain_v, w1, w2, out_v, rows, target)
        final[0] = w1[...].astype(B16)
        final[1] = w2[...].astype(B16)
        back = [
            pltpu.make_async_copy(final, state_out, sems.at[0]),
            pltpu.make_async_copy(out_v, out.at[:, pl.ds(first_pair * 128, pairs * 128)], sems.at[1]),
        ]
        for move in back:
            move.start()
        for move in back:
            move.wait()


ANYWHERE = pl.BlockSpec(memory_space=pl.ANY)
MOST = 56 << 20


def run_chain(turn, first_pair, where, qkv, rate, gain, state, out):
    tokens = sum(part.shape[0] for part in qkv)
    heads = rate[0].shape[1]
    pairs = state.shape[1]
    batches = tokens // MB
    operands = [where, *qkv, *rate, gain, state] + ([] if out is None else [out])
    return pl.pallas_call(
        functools.partial(chain_kernel, pairs, first_pair, batches, turn),
        out_shape=[
            jax.ShapeDtypeStruct((tokens, heads * 64), B16),
            jax.ShapeDtypeStruct(state.shape, B16),
        ],
        in_specs=[pl.BlockSpec(memory_space=pltpu.SMEM)] + [ANYWHERE] * (len(operands) - 1),
        out_specs=[ANYWHERE, ANYWHERE],
        scratch_shapes=[
            pltpu.VMEM((tokens, pairs * 384), F32),
            pltpu.VMEM((batches, heads, MB), F32),
            pltpu.VMEM((pairs,) + gain.shape[1:], F32),
            pltpu.VMEM(state.shape, state.dtype),
            pltpu.VMEM(state.shape, B16),
            pltpu.VMEM((tokens, pairs * 128), B16),
            pltpu.VMEM(state.shape[1:], F32),
            pltpu.VMEM(state.shape[1:], F32),
            pltpu.VMEM((pairs, 256, 128), B16),
            pltpu.VMEM((pairs, 64, 128), F32),
            pltpu.SemaphoreType.DMA((6,)),
        ],
        input_output_aliases={} if out is None else {7: 0},
        compiler_params=pltpu.CompilerParams(vmem_limit_bytes=MOST),
        cost_estimate=pl.CostEstimate(flops=10**9, bytes_accessed=30 * 10**6, transcendentals=0),
        name=f"chain_{turn}",
    )(*operands)


def project_kernel(count, *refs):
    blocks = refs[:count]
    weight, rate_weight, base, out, rate, rows, sems = refs[count:]

    @pl.when(pl.program_id(0) == 0)
    def _():
        moves = [pltpu.make_async_copy(b, rows.at[pl.ds(i * MB, MB)], sems.at[i]) for i, b in enumerate(blocks)]
        for move in moves:
            move.start()
        for move in moves:
            move.wait()
        gate = dot(rows[...], rate_weight[0]).T
        gate = base[0] * jax.nn.sigmoid(gate)
        for i in range(count):
            rate[i] = gate[:, i * MB : (i + 1) * MB]

    out[...] = dot(rows[...], weight[0])


def project(blocks, layer, qkv_weight, rate_weight, base):
    count = len(blocks)
    depth, columns = qkv_weight.shape[1:]
    heads = rate_weight.shape[2]
    tile = 384
    return pl.pallas_call(
        functools.partial(project_kernel, count),
        grid=(columns // tile,),
        out_shape=[
            jax.ShapeDtypeStruct((count * MB, columns), F32),
            jax.ShapeDtypeStruct((count, heads, MB), F32),
        ],
        in_specs=[ANYWHERE] * count
        + [
            pl.BlockSpec((1, depth, tile), lambda i: (layer, 0, i)),
            pl.BlockSpec((1, depth, heads), lambda i: (layer, 0, 0)),
            pl.BlockSpec((1, heads, 1), lambda i: (layer, 0, 0)),
        ],
        out_specs=[
            pl.BlockSpec((count * MB, tile), lambda i: (0, i)),
            pl.BlockSpec((count, heads, MB), lambda i: (0, 0, 0)),
        ],
        scratch_shapes=[pltpu.VMEM((count * MB, depth), B16), pltpu.SemaphoreType.DMA((count,))],
        compiler_params=pltpu.CompilerParams(vmem_limit_bytes=MOST),
        cost_estimate=pl.CostEstimate(flops=2 * count * MB * depth * columns, bytes_accessed=depth * columns * 2, transcendentals=0),
        name="project",
    )(*blocks, qkv_weight, rate_weight, base)


def unproject_kernel(count, left, right, *outs):
    total = dot(left[...], right[0]).astype(B16)
    for i in range(count):
        outs[i][...] = total[i * MB : (i + 1) * MB]


def unproject(mixed, first, count, layer, out_weight):
    depth, columns = out_weight.shape[1:]
    tile = 1024
    return pl.pallas_call(
        functools.partial(unproject_kernel, count),
        grid=(columns // tile,),
        out_shape=[jax.ShapeDtypeStruct((MB, columns), B16)] * count,
        in_specs=[
            pl.BlockSpec((count * MB, depth), lambda i: (0, 0)),
            pl.BlockSpec((1, depth, tile), lambda i: (layer, 0, i)),
        ],
        out_specs=[pl.BlockSpec((MB, tile), lambda i: (0, i))] * count,
        compiler_params=pltpu.CompilerParams(vmem_limit_bytes=MOST),
        cost_estimate=pl.CostEstimate(flops=2 * count * MB * depth * columns, bytes_accessed=depth * columns * 2, transcendentals=0),
        name="unproject",
    )(mixed[first * MB : (first + count) * MB], out_weight)


NEAR = [(0, 0), (0, 1), (1, 0), (3, 0), (2, 0)]
FAR = [(1, 1), (3, 1), (2, 1)]
SLOTS = NEAR + FAR


def send(block, dx, dz):
    route = [(2 * x + z, 2 * ((x + dx) % 4) + (z ^ dz)) for x in range(4) for z in range(2)]
    return lax.ppermute(block, "head", route)


def fetch(block, dx, dz):
    return send(block, -dx, dz)


def gather_near(own):
    return [own] + [fetch(own, dx, dz) for dx, dz in NEAR[1:]]


def gather_far(near):
    return [fetch(near[1], 1, 0), fetch(near[1], 3, 0), fetch(near[4], 0, 1)]


def add(*blocks):
    return sum(block.astype(F32) for block in blocks)


def body(tokens, norm_gain, qkv_weight, rate_weight, rate_base, fast_first, fast_second, inner_gain, out_weight):
    seq_count = lax.axis_size("seq")
    layers, heads = rate_base.shape
    pairs = heads // 2
    me = lax.axis_index("head")
    batch = jnp.arange(len(SLOTS))
    offset = (batch // 2 - me // 2) % 4 * 2 + (batch + me) % 2
    table = jnp.array([SLOTS.index((dx, dz)) for dx in range(4) for dz in range(2)])
    where = jnp.concatenate([lax.axis_index("seq").reshape(1), table[offset]]).astype(jnp.int32)

    def turned(weights):
        return weights.reshape(layers, pairs, 128, 256).swapaxes(2, 3)

    initial = jnp.stack([turned(fast_first), turned(fast_second)], axis=1)
    gains = jnp.repeat(inner_gain.reshape(layers, pairs, 2, 64).swapaxes(2, 3), MB, axis=3)
    base = (rate_base * (1.0 / MB))[:, :, None]
    stream = tokens.astype(F32)
    for layer in range(layers):
        mean_square = jnp.mean(stream * stream, axis=-1, keepdims=True)
        normed = (stream * lax.rsqrt(mean_square + 1e-06) * norm_gain[layer]).astype(B16)
        near = gather_near(normed)
        far = gather_far(near)
        parts = [project(blocks, layer, qkv_weight, rate_weight, base) for blocks in (near, far)]
        qkv, rate = zip(*parts)
        mixed = None
        states = [initial[layer][:, list(group)] for group in GROUPS]
        for turn in range(seq_count):
            for i, group in enumerate(GROUPS):
                mixed, state = run_chain(turn, group[0], where, qkv, rate, gains[layer], states[i], mixed)
                if turn < seq_count - 1:
                    states[i] = lax.ppermute(state, "seq", [(turn, turn + 1)])
        part_far = unproject(mixed, len(NEAR), len(FAR), layer, out_weight)
        part = unproject(mixed, 0, len(NEAR), layer, out_weight)
        a, b, c = send(part_far[0], 1, 0), send(part_far[1], 3, 0), send(part_far[2], 0, 1)
        side = add(part[1], a, b).astype(B16)
        across = add(part[4], c).astype(B16)
        side, across, left, right = lax.optimization_barrier((side, across, part[2], part[3]))
        sums = [part[0], send(left, 1, 0), send(right, 3, 0), send(across, 2, 0), send(side, 0, 1)]
        out = (stream + add(*sums)).astype(B16)
        stream = out.astype(F32)
    return out


GROUPS = [(0, 1, 2)]


def solution(mesh):
    rows = P(("dp", "seq", "head"), None)
    in_specs = (
        rows,
        P(),
        P(None, None, "head"),
        P(None, None, "head"),
        P(None, "head"),
        P(None, "head", None, None),
        P(None, "head", None, None),
        P(None, "head", None),
        P(None, "head", None),
    )
    return jax.shard_map(body, mesh=mesh, in_specs=in_specs, out_specs=rows, check_vma=False)
```

time: 329 us -> 293 us (0.89)
  blocking collectives: 80.3 us -> 0 us
  Pallas kernels: 40 us -> 83.3 us
  starting transfers between devices: 16.7 us -> 56 us
  waiting for transfers between devices: 150 us -> 119 us
  local copies, waits for them, and re-layouts: 31 us -> 22.3 us
  other arithmetic: 7.22 us -> 11 us
    all_to_all x2 -> x0, blocking collectives: 80.3 us -> none  [body(): parts = lax.all_to_all(parts, 'head', 0, 0, tiled=True)]
    all_to_all x2 -> x0, waiting for transfers between devices: 77.9 us -> none  [to_head_order(): lax.all_to_all(jnp.broadcast_to(block[None], (count,) + block.shape), 'he...]
    ppermute x6 -> x34, starting transfers between devices: 5.33 us -> 56 us  [the longest x28 50.6 us: send(): return lax.ppermute(block, 'head', route)]
    ppermute x6 -> x34, waiting for transfers between devices: 72.2 us -> 119 us  [the longest x6 78.1 us: body(): states[i] = lax.ppermute(state, 'seq', [(turn, turn + 1)])]
    pallas_call x12 -> x16, Pallas kernels: 40 us -> 83.3 us  [the longest x4 34.9 us: project(): pl.pallas_call(functools.partial(project_kernel, count), grid=(columns //...]
    all_to_all x2 -> x0, starting transfers between devices: 11.4 us -> none  [to_head_order(): lax.all_to_all(jnp.broadcast_to(block[None], (count,) + block.shape), 'he...]
    unnamed x28 -> x53, local copies, waits for them, and re-layouts: 19.9 us -> 8.63 us
    slice x4 -> x7, local copies, waits for them, and re-layouts: 0.34 us -> 5.64 us  [the longest x4 4.64 us: unproject(): mixed[first * MB:(first + count) * MB]]
  transfers between devices with their start and end apart: 8 -> 34, of which waited for: 4 -> 16; matrix products, arithmetic and copies ran while one was open for 3% -> 5% of each run, Pallas kernels for 0% -> 9%
where the time goes in v2:
time: 293 us; the launch traced here: 292 us
  waiting for transfers between devices  119 us (41%)
  Pallas kernels  83.3 us (28%)
  starting transfers between devices  56 us (19%)
  local copies, waits for them, and re-layouts  22.3 us (8%)
  other arithmetic  11 us (4%)
    ppermute x6, waiting for transfers between devices, body(): states[i] = lax.ppermute(state, 'seq', [(turn, turn + 1)])  78.1 us
    ppermute x28, starting transfers between devices, send(): return lax.ppermute(block, 'head', route)  50.6 us
    ppermute x28, waiting for transfers between devices, send(): return lax.ppermute(block, 'head', route)  40.9 us
    pallas_call x4, Pallas kernels, project(): pl.pallas_call(functools.partial(project_kernel, count), grid=(columns //...  34.9 us
    pallas_call x8, Pallas kernels, run_chain(): pl.pallas_call(functools.partial(chain_kernel, pairs, first_pair, batches...  32 us
    pallas_call x4, Pallas kernels, unproject(): pl.pallas_call(functools.partial(unproject_kernel, count), grid=(columns...  16.4 us
    unnamed x53, local copies, waits for them, and re-layouts  8.63 us
  transfers between devices with their start and end apart: 34, of which 16 were waited for; matrix products, arithmetic and copies ran while one was open for 5% of the time, Pallas kernels for 9%

profile of v2, /device:TPU:24, one launch (start us, length us, event | category | flops | bytes accessed | tf_op | source)
XLA Modules:
  0.0 292.2 jit_solution(4446396917332071828)
XLA Ops:
  0.8 1.2 fusion
  2.0 2.0 fusion.2.refs_0_
  4.0 3.9 %collective-permute-start = (bf16[64,3072]{1,0:T(8,128)(2,1)}, bf16[64,3072]{1,0:T(8,128)(2,1)}, u32[]{:S(2)}, u32[]{:S(2)}) collective-permute-start(bf16[64,3072]{1,0:T(8,128)(2,1)} %fusion.2.refs_0_), channel_id=1, source_target_pairs={{0,4},{4,0},{8,12},{12,8},{16,20},{20,16},{24,28},{28,24},{1,5},{5... | collective-permute-start | bytes 1179656 | tf_op jit(solution)/shard_map/ppermute | solution.py:285
  7.9 3.0 %collective-permute-start.3 = (bf16[64,3072]{1,0:T(8,128)(2,1)}, bf16[64,3072]{1,0:T(8,128)(2,1)}, u32[]{:S(2)}, u32[]{:S(2)}) collective-permute-start(bf16[64,3072]{1,0:T(8,128)(2,1)} %fusion.2.refs_0_), channel_id=1, source_target_pairs={{0,16},{4,20},{8,24},{12,28},{16,0},{20,4},{24,8},{28,12},{1,17},{... | collective-permute-start | bytes 1179656 | tf_op jit(solution)/shard_map/ppermute | solution.py:285
  10.9 1.1 collective-permute-start.1
  12.1 0.9 collective-permute-start.2
  14.4 2.4 copy.41.refs_6_.refs_4_
  20.0 1.0 copy.58
  21.0 2.4 collective-permute-start.4
  24.8 5.5 %collective-permute-done.1.refs_2_ = bf16[64,3072]{1,0:T(8,128)(2,1)} collective-permute-done((bf16[64,3072]{1,0:T(8,128)(2,1)}, bf16[64,3072]{1,0:T(8,128)(2,1)}, u32[]{:S(2)}, u32[]{:S(2)}) %collective-permute-start.1) | collective-permute-done | bytes 393248 | tf_op jit(solution)/shard_map/ppermute | solution.py:285
  30.3 9.4 %project.4 = (f32[320,1152]{1,0:T(8,128)}, f32[5,6,64]{2,1,0:T(8,128)}) custom-call(bf16[64,3072]{1,0:T(8,128)(2,1)} %fusion.2.refs_0_, bf16[64,3072]{1,0:T(8,128)(2,1)} %collective-permute-done.refs_1_, bf16[64,3072]{1,0:T(8,128)(2,1)} %collective-permute-done.1.refs_2_, bf16[64,3072]{1,0:T(8,128)(2,1)} %collective-permute-done.2.refs_3_, ...), custom_call_target="tpu_custom_call" | custom-call | flops 2264924160 | bytes 7077888 | tf_op jit(solution)/shard_map/project/pallas_call | solution.py:230
  41.4 8.1 %project.5 = (f32[192,1152]{1,0:T(8,128)}, f32[3,6,64]{2,1,0:T(8,128)}) custom-call(bf16[64,3072]{1,0:T(8,128)(2,1)} %copy-done.12, bf16[64,3072]{1,0:T(8,128)(2,1)} %copy-done.13, bf16[64,3072]{1,0:T(8,128)(2,1)} %copy-done.14, bf16[2,3072,1152]{2,1,0:T(8,128)(2,1)} %refs_3_.3, bf16[2,3072,6]{2,1,0:T(8,128)(2,1)} %copy.41.refs_6_.refs_4_, ...), custom_call_target="tpu_custom_call" | custom-call | flops 1358954496 | bytes 7077888 | tf_op jit(solution)/shard_map/project/pallas_call | solution.py:230
  54.5 1.3 collective-permute-start.9
  55.8 63.3 %collective-permute-done.9.state = bf16[2,3,256,128]{3,2,1,0:T(8,128)(2,1)S(1)} collective-permute-done((bf16[2,3,256,128]{3,2,1,0:T(8,128)(2,1)}, bf16[2,3,256,128]{3,2,1,0:T(8,128)(2,1)S(1)}, u32[]{:S(2)}, u32[]{:S(2)}) %collective-permute-start.9) | collective-permute-done | bytes 393248 | tf_op jit(solution)/shard_map/ppermute | solution.py:334
  119.9 13.8 %chain_3.2 = (bf16[512,384]{1,0:T(8,128)(2,1)}, bf16[2,3,256,128]{3,2,1,0:T(8,128)(2,1)}) custom-call(s32[9]{0:T(128)} %pad_add_fusion.where, f32[320,1152]{1,0:T(8,128)} %get-tuple-element.51.qkv_a, f32[192,1152]{1,0:T(8,128)} %get-tuple-element.52.qkv_b, f32[5,6,64]{2,1,0:T(8,128)} %get-tuple-element.53.rate_a, ...), custom_call_target="tpu_custom_call", output_to_operand_aliasing={{0}: (7, {})} | custom-call | flops 1000000000 | bytes 30000000 | tf_op jit(solution)/shard_map/chain_3/pallas_call | solution.py:178
  133.7 1.6 slice.49.left
  135.3 3.9 %unproject.5 = (bf16[64,3072]{1,0:T(8,128)(2,1)}, bf16[64,3072]{1,0:T(8,128)(2,1)}, bf16[64,3072]{1,0:T(8,128)(2,1)}) custom-call(bf16[192,384]{1,0:T(8,128)(2,1)} %slice.49.left, bf16[2,384,3072]{2,1,0:T(8,128)(2,1)} %right.7), custom_call_target="tpu_custom_call" | custom-call | flops 452984832 | bytes 2359296 | tf_op jit(solution)/shard_map/unproject/pallas_call | solution.py:263
  139.2 0.9 collective-permute-start.12
  140.9 1.7 collective-permute-start.10
  142.6 3.7 %collective-permute-start.11 = (bf16[64,3072]{1,0:T(8,128)(2,1)}, bf16[64,3072]{1,0:T(8,128)(2,1)S(1)}, u32[]{:S(2)}, u32[]{:S(2)}) collective-permute-start(bf16[64,3072]{1,0:T(8,128)(2,1)} %get-tuple-element.65), channel_id=1, source_target_pairs={{0,24},{4,28},{8,0},{12,4},{16,8},{20,12},{24,16},{28,20},{1,25},{... | collective-permute-start | bytes 1179656 | tf_op jit(solution)/shard_map/ppermute | solution.py:285
  146.3 4.3 %unproject.4 = (bf16[64,3072]{1,0:T(8,128)(2,1)}, bf16[64,3072]{1,0:T(8,128)(2,1)}, bf16[64,3072]{1,0:T(8,128)(2,1)}, bf16[64,3072]{1,0:T(8,128)(2,1)}, bf16[64,3072]{1,0:T(8,128)(2,1)}) custom-call(bf16[320,384]{1,0:T(8,128)(2,1)} %slice.48.left, bf16[2,384,3072]{2,1,0:T(8,128)(2,1)} %right.7), custom_call_target="tpu_custom_call" | custom-call | flops 754974720 | bytes 2359296 | tf_op jit(solution)/shard_map/unproject/pallas_call | solution.py:263
  150.6 1.2 add_convert_fusion.2
  151.8 1.8 collective-permute-done.10
  153.7 1.1 add_convert_fusion.3
  154.8 1.2 collective-permute-start.13
  156.0 2.6 collective-permute-start.14
  158.6 1.4 collective-permute-start.15
  160.0 3.1 %collective-permute-start.16 = (bf16[64,3072]{1,0:T(8,128)(2,1)S(1)}, bf16[64,3072]{1,0:T(8,128)(2,1)S(1)}, u32[]{:S(2)}, u32[]{:S(2)}) collective-permute-start(bf16[64,3072]{1,0:T(8,128)(2,1)S(1)} %add_convert_fusion.3), channel_id=1, source_target_pairs={{0,4},{4,0},{8,12},{12,8},{16,20},{20,16},{24,28},{28,24},{1,5},{5... | collective-permute-start | bytes 1179656 | tf_op jit(solution)/shard_map/ppermute | solution.py:285
  163.1 4.5 %collective-permute-done.13 = bf16[64,3072]{1,0:T(8,128)(2,1)S(1)} collective-permute-done((bf16[64,3072]{1,0:T(8,128)(2,1)S(1)}, bf16[64,3072]{1,0:T(8,128)(2,1)S(1)}, u32[]{:S(2)}, u32[]{:S(2)}) %collective-permute-start.13) | collective-permute-done | bytes 393248 | tf_op jit(solution)/shard_map/ppermute | solution.py:285
  167.6 5.1 %collective-permute-done.14 = bf16[64,3072]{1,0:T(8,128)(2,1)S(1)} collective-permute-done((bf16[64,3072]{1,0:T(8,128)(2,1)S(1)}, bf16[64,3072]{1,0:T(8,128)(2,1)S(1)}, u32[]{:S(2)}, u32[]{:S(2)}) %collective-permute-start.14) | collective-permute-done | bytes 393248 | tf_op jit(solution)/shard_map/ppermute | solution.py:285
  172.8 1.8 collective-permute-done.15
  175.3 2.4 collective-permute-start.17
  178.0 3.4 %collective-permute-start.18 = (bf16[64,3072]{1,0:T(8,128)(2,1)S(1)}, bf16[64,3072]{1,0:T(8,128)(2,1)S(1)}, u32[]{:S(2)}, u32[]{:S(2)}) collective-permute-start(bf16[64,3072]{1,0:T(8,128)(2,1)S(1)} %fusion.6.refs_0_), channel_id=1, source_target_pairs={{0,24},{4,28},{8,0},{12,4},{16,8},{20,12},{24,16},{28,20},{1,25},{... | collective-permute-start | bytes 1179656 | tf_op jit(solution)/shard_map/ppermute | solution.py:285
  181.5 3.1 %collective-permute-done.17.refs_1_ = bf16[64,3072]{1,0:T(8,128)(2,1)S(1)} collective-permute-done((bf16[64,3072]{1,0:T(8,128)(2,1)S(1)}, bf16[64,3072]{1,0:T(8,128)(2,1)S(1)}, u32[]{:S(2)}, u32[]{:S(2)}) %collective-permute-start.17) | collective-permute-done | bytes 393248 | tf_op jit(solution)/shard_map/ppermute | solution.py:285
  184.6 1.9 collective-permute-start.21
  186.7 4.6 %collective-permute-done.20.refs_4_ = bf16[64,3072]{1,0:T(8,128)(2,1)S(1)} collective-permute-done((bf16[64,3072]{1,0:T(8,128)(2,1)S(1)}, bf16[64,3072]{1,0:T(8,128)(2,1)S(1)}, u32[]{:S(2)}, u32[]{:S(2)}) %collective-permute-start.20) | collective-permute-done | bytes 393248 | tf_op jit(solution)/shard_map/ppermute | solution.py:285
  191.2 1.2 collective-permute-start.23
  194.3 1.0 copy.57
  195.3 1.2 collective-permute-done.18.refs_2_
  196.5 0.8 collective-permute-done.19.refs_3_
  197.3 9.4 %project.6 = (f32[320,1152]{1,0:T(8,128)}, f32[5,6,64]{2,1,0:T(8,128)}) custom-call(bf16[64,3072]{1,0:T(8,128)(2,1)} %copy-done.2, bf16[64,3072]{1,0:T(8,128)(2,1)} %copy-done.9, bf16[64,3072]{1,0:T(8,128)(2,1)} %copy-done.11, bf16[64,3072]{1,0:T(8,128)(2,1)} %collective-permute-done.19.refs_3_, bf16[64,3072]{1,0:T(8,128)(2,1)} %copy-done.10, ...), custom_call_target="tpu_custom_call" | custom-call | flops 2264924160 | bytes 7077888 | tf_op jit(solution)/shard_map/project/pallas_call | solution.py:230
  206.8 8.1 %project.7 = (f32[192,1152]{1,0:T(8,128)}, f32[3,6,64]{2,1,0:T(8,128)}) custom-call(bf16[64,3072]{1,0:T(8,128)(2,1)} %collective-permute-done.21.refs_0_, bf16[64,3072]{1,0:T(8,128)(2,1)} %collective-permute-done.22.refs_1_, bf16[64,3072]{1,0:T(8,128)(2,1)} %collective-permute-done.23.refs_2_, bf16[2,3072,1152]{2,1,0:T(8,128)(2,1)} %refs_3_.3, ...), custom_call_target="tpu_custom_call" | custom-call | flops 1358954496 | bytes 7077888 | tf_op jit(solution)/shard_map/project/pallas_call | solution.py:230
  214.8 0.9 chain_0.3
  220.2 1.3 collective-permute-start.26
  221.5 14.8 %collective-permute-done.26.state = bf16[2,3,256,128]{3,2,1,0:T(8,128)(2,1)S(1)} collective-permute-done((bf16[2,3,256,128]{3,2,1,0:T(8,128)(2,1)}, bf16[2,3,256,128]{3,2,1,0:T(8,128)(2,1)S(1)}, u32[]{:S(2)}, u32[]{:S(2)}) %collective-permute-start.26) | collective-permute-done | bytes 393248 | tf_op jit(solution)/shard_map/ppermute | solution.py:334
  237.0 13.6 %chain_3.3 = (bf16[512,384]{1,0:T(8,128)(2,1)}, bf16[2,3,256,128]{3,2,1,0:T(8,128)(2,1)}) custom-call(s32[9]{0:T(128)} %pad_add_fusion.where, f32[320,1152]{1,0:T(8,128)} %get-tuple-element.74.qkv_a, f32[192,1152]{1,0:T(8,128)} %get-tuple-element.75.qkv_b, f32[5,6,64]{2,1,0:T(8,128)} %get-tuple-element.76.rate_a, ...), custom_call_target="tpu_custom_call", output_to_operand_aliasing={{0}: (7, {})} | custom-call | flops 1000000000 | bytes 30000000 | tf_op jit(solution)/shard_map/chain_3/pallas_call | solution.py:178
  250.7 1.6 slice.55.left
  252.2 3.9 %unproject.7 = (bf16[64,3072]{1,0:T(8,128)(2,1)}, bf16[64,3072]{1,0:T(8,128)(2,1)}, bf16[64,3072]{1,0:T(8,128)(2,1)}) custom-call(bf16[192,384]{1,0:T(8,128)(2,1)} %slice.55.left, bf16[2,384,3072]{2,1,0:T(8,128)(2,1)} %right.7), custom_call_target="tpu_custom_call" | custom-call | flops 452984832 | bytes 2359296 | tf_op jit(solution)/shard_map/unproject/pallas_call | solution.py:263
  256.2 1.2 collective-permute-start.29
  258.1 1.0 collective-permute-start.27
  259.1 2.3 collective-permute-start.28
  261.4 4.3 %unproject.6 = (bf16[64,3072]{1,0:T(8,128)(2,1)}, bf16[64,3072]{1,0:T(8,128)(2,1)}, bf16[64,3072]{1,0:T(8,128)(2,1)}, bf16[64,3072]{1,0:T(8,128)(2,1)}, bf16[64,3072]{1,0:T(8,128)(2,1)}) custom-call(bf16[320,384]{1,0:T(8,128)(2,1)} %slice.54.left, bf16[2,384,3072]{2,1,0:T(8,128)(2,1)} %right.7), custom_call_target="tpu_custom_call" | custom-call | flops 754974720 | bytes 2359296 | tf_op jit(solution)/shard_map/unproject/pallas_call | solution.py:263
  265.7 1.2 add_convert_fusion
  266.9 3.8 %collective-permute-done.27 = bf16[64,3072]{1,0:T(8,128)(2,1)S(1)} collective-permute-done((bf16[64,3072]{1,0:T(8,128)(2,1)}, bf16[64,3072]{1,0:T(8,128)(2,1)S(1)}, u32[]{:S(2)}, u32[]{:S(2)}) %collective-permute-start.27) | collective-permute-done | bytes 393248 | tf_op jit(solution)/shard_map/ppermute | solution.py:285
  270.7 1.3 collective-permute-done.28
  272.0 1.1 add_convert_fusion.1
  273.1 1.5 collective-permute-start.30
  274.6 5.1 %collective-permute-start.31 = (bf16[64,3072]{1,0:T(8,128)(2,1)S(1)}, bf16[64,3072]{1,0:T(8,128)(2,1)S(1)}, u32[]{:S(2)}, u32[]{:S(2)}) collective-permute-start(bf16[64,3072]{1,0:T(8,128)(2,1)S(1)} %copy-done.17), channel_id=1, source_target_pairs={{0,24},{4,28},{8,0},{12,4},{16,8},{20,12},{24,16},{28,20},{1,25},{... | collective-permute-start | bytes 1179656 | tf_op jit(solution)/shard_map/ppermute | solution.py:285
  279.8 1.4 collective-permute-start.32
  281.2 2.8 collective-permute-start.33
  284.0 1.5 collective-permute-done.30
  285.4 3.8 %collective-permute-done.31 = bf16[64,3072]{1,0:T(8,128)(2,1)S(1)} collective-permute-done((bf16[64,3072]{1,0:T(8,128)(2,1)S(1)}, bf16[64,3072]{1,0:T(8,128)(2,1)S(1)}, u32[]{:S(2)}, u32[]{:S(2)}) %collective-permute-start.31) | collective-permute-done | bytes 393248 | tf_op jit(solution)/shard_map/ppermute | solution.py:285
  289.3 1.8 collective-permute-done.32
  291.1 1.1 fusion.7
  (111 shorter events, 23.9 us)
Async XLA Ops:
  2.0 16.7 %copy-start.3 = (f32[2,6,64,256]{3,2,1,0:T(8,128)S(1)}, f32[2,6,64,256]{3,2,1,0:T(8,128)}, u32[]{:S(2)}) copy-start(f32[2,6,64,256]{3,2,1,0:T(8,128)} %param.18) | copy-start | bytes 2359300
  4.0 17.0 %collective-permute-start = (bf16[64,3072]{1,0:T(8,128)(2,1)}, bf16[64,3072]{1,0:T(8,128)(2,1)}, u32[]{:S(2)}, u32[]{:S(2)}) collective-permute-start(bf16[64,3072]{1,0:T(8,128)(2,1)} %fusion.2.refs_0_), channel_id=1, source_target_pairs={{0,4},{4,0},{8,12},{12,8},{16,20},{20,16},{24,28},{28,24},{1,5},{5... | collective-permute-start | bytes 1179656 | tf_op jit(solution)/shard_map/ppermute | solution.py:285
  7.9 15.5 %collective-permute-start.3 = (bf16[64,3072]{1,0:T(8,128)(2,1)}, bf16[64,3072]{1,0:T(8,128)(2,1)}, u32[]{:S(2)}, u32[]{:S(2)}) collective-permute-start(bf16[64,3072]{1,0:T(8,128)(2,1)} %fusion.2.refs_0_), channel_id=1, source_target_pairs={{0,16},{4,20},{8,24},{12,28},{16,0},{20,4},{24,8},{28,12},{1,17},{... | collective-permute-start | bytes 1179656 | tf_op jit(solution)/shard_map/ppermute | solution.py:285
  10.9 19.4 %collective-permute-start.1 = (bf16[64,3072]{1,0:T(8,128)(2,1)}, bf16[64,3072]{1,0:T(8,128)(2,1)}, u32[]{:S(2)}, u32[]{:S(2)}) collective-permute-start(bf16[64,3072]{1,0:T(8,128)(2,1)} %fusion.2.refs_0_), channel_id=1, source_target_pairs={{0,24},{4,28},{8,0},{12,4},{16,8},{20,12},{24,16},{28,20},{1,25},{... | collective-permute-start | bytes 1179656 | tf_op jit(solution)/shard_map/ppermute | solution.py:285
  12.1 18.3 %collective-permute-start.2 = (bf16[64,3072]{1,0:T(8,128)(2,1)}, bf16[64,3072]{1,0:T(8,128)(2,1)}, u32[]{:S(2)}, u32[]{:S(2)}) collective-permute-start(bf16[64,3072]{1,0:T(8,128)(2,1)} %fusion.2.refs_0_), channel_id=1, source_target_pairs={{0,8},{4,12},{8,16},{12,20},{16,24},{20,28},{24,0},{28,4},{1,9},{5... | collective-permute-start | bytes 1179656 | tf_op jit(solution)/shard_map/ppermute | solution.py:285
  14.4 4.6 %copy-start.4 = (f32[2,6,64,256]{3,2,1,0:T(8,128)S(1)}, f32[2,6,64,256]{3,2,1,0:T(8,128)}, u32[]{:S(2)}) copy-start(f32[2,6,64,256]{3,2,1,0:T(8,128)} %param.17) | copy-start | bytes 2359300
  19.4 1.6 copy-start.15
  19.4 4.1 %copy-start = (s32[8]{0:T(128)S(1)}, s32[8]{0:T(128)}, u32[]{:S(2)}) copy-start(s32[8]{0:T(128)} %constant.79.clone) | copy-start | bytes 100
  21.0 18.7 %collective-permute-start.4 = (bf16[64,3072]{1,0:T(8,128)(2,1)}, bf16[64,3072]{1,0:T(8,128)(2,1)S(1)}, u32[]{:S(2)}, u32[]{:S(2)}) collective-permute-start(bf16[64,3072]{1,0:T(8,128)(2,1)} %collective-permute-done.refs_1_), channel_id=1, source_target_pairs={{0,24},{4,28},{8,0},{12,4},{16,8},{20,12},{24,16},{28,20},{1,25},{... | collective-permute-start | bytes 1179656 | tf_op jit(solution)/shard_map/ppermute | solution.py:285
  23.4 16.3 %collective-permute-start.5 = (bf16[64,3072]{1,0:T(8,128)(2,1)}, bf16[64,3072]{1,0:T(8,128)(2,1)S(1)}, u32[]{:S(2)}, u32[]{:S(2)}) collective-permute-start(bf16[64,3072]{1,0:T(8,128)(2,1)} %collective-permute-done.refs_1_), channel_id=1, source_target_pairs={{0,8},{4,12},{8,16},{12,20},{16,24},{20,28},{24,0},{28,4},{1,9},{5... | collective-permute-start | bytes 1179656 | tf_op jit(solution)/shard_map/ppermute | solution.py:285
  23.4 16.3 %collective-permute-start.6 = (bf16[64,3072]{1,0:T(8,128)(2,1)}, bf16[64,3072]{1,0:T(8,128)(2,1)S(1)}, u32[]{:S(2)}, u32[]{:S(2)}) collective-permute-start(bf16[64,3072]{1,0:T(8,128)(2,1)} %collective-permute-done.3.refs_4_), channel_id=1, source_target_pairs={{0,4},{4,0},{8,12},{12,8},{16,20},{20,16},{24,28},{28,24},{1,5},{5... | collective-permute-start | bytes 1179656 | tf_op jit(solution)/shard_map/ppermute | solution.py:285
  39.7 0.7 copy-start.12
  39.8 0.9 copy-start.13
  40.6 0.7 copy-start.14
  50.2 0.7 collective-permute-start.7
  50.9 0.8 copy-start.22
  52.4 0.7 collective-permute-start.8
  53.1 0.8 copy-start.23
  54.5 64.6 %collective-permute-start.9 = (bf16[2,3,256,128]{3,2,1,0:T(8,128)(2,1)}, bf16[2,3,256,128]{3,2,1,0:T(8,128)(2,1)S(1)}, u32[]{:S(2)}, u32[]{:S(2)}) collective-permute-start(bf16[2,3,256,128]{3,2,1,0:T(8,128)(2,1)} %get-tuple-element.59), channel_id=1, source_target_pairs={{64,96},{65,97},{66,98},{67,99},{68,100},{69,101},{70,102},{71,103... | collective-permute-start | bytes 1179656 | tf_op jit(solution)/shard_map/ppermute | solution.py:334
  119.2 0.8 copy-start.21
  135.3 4.8 %copy-start.5 = (bf16[512,384]{1,0:T(8,128)(2,1)S(1)}, bf16[512,384]{1,0:T(8,128)(2,1)}, u32[]{:S(2)}) copy-start(bf16[512,384]{1,0:T(8,128)(2,1)} %get-tuple-element.61) | copy-start | bytes 1179652
  139.2 11.4 %collective-permute-start.12 = (bf16[64,3072]{1,0:T(8,128)(2,1)}, bf16[64,3072]{1,0:T(8,128)(2,1)S(1)}, u32[]{:S(2)}, u32[]{:S(2)}) collective-permute-start(bf16[64,3072]{1,0:T(8,128)(2,1)} %get-tuple-element.67), channel_id=1, source_target_pairs={{0,4},{4,0},{8,12},{12,8},{16,20},{20,16},{24,28},{28,24},{1,5},{5... | collective-permute-start | bytes 1179656 | tf_op jit(solution)/shard_map/ppermute | solution.py:285
  140.9 12.7 %collective-permute-start.10 = (bf16[64,3072]{1,0:T(8,128)(2,1)}, bf16[64,3072]{1,0:T(8,128)(2,1)S(1)}, u32[]{:S(2)}, u32[]{:S(2)}) collective-permute-start(bf16[64,3072]{1,0:T(8,128)(2,1)} %get-tuple-element.64), channel_id=1, source_target_pairs={{0,8},{4,12},{8,16},{12,20},{16,24},{20,28},{24,0},{28,4},{1,9},{5... | collective-permute-start | bytes 1179656 | tf_op jit(solution)/shard_map/ppermute | solution.py:285
  142.6 11.1 %collective-permute-start.11 = (bf16[64,3072]{1,0:T(8,128)(2,1)}, bf16[64,3072]{1,0:T(8,128)(2,1)S(1)}, u32[]{:S(2)}, u32[]{:S(2)}) collective-permute-start(bf16[64,3072]{1,0:T(8,128)(2,1)} %get-tuple-element.65), channel_id=1, source_target_pairs={{0,24},{4,28},{8,0},{12,4},{16,8},{20,12},{24,16},{28,20},{1,25},{... | collective-permute-start | bytes 1179656 | tf_op jit(solution)/shard_map/ppermute | solution.py:285
  150.6 4.2 %copy-start.18 = (bf16[64,3072]{1,0:T(8,128)(2,1)S(1)}, bf16[64,3072]{1,0:T(8,128)(2,1)}, u32[]{:S(2)}) copy-start(bf16[64,3072]{1,0:T(8,128)(2,1)} %get-tuple-element.70) | copy-start | bytes 1179652
  150.6 5.4 %copy-start.16 = (bf16[64,3072]{1,0:T(8,128)(2,1)S(1)}, bf16[64,3072]{1,0:T(8,128)(2,1)}, u32[]{:S(2)}) copy-start(bf16[64,3072]{1,0:T(8,128)(2,1)} %get-tuple-element.71) | copy-start | bytes 1179652
  150.6 24.0 %copy-start.1 = (bf16[64,3072]{1,0:T(8,128)(2,1)S(1)}, bf16[64,3072]{1,0:T(8,128)(2,1)}, u32[]{:S(2)}) copy-start(bf16[64,3072]{1,0:T(8,128)(2,1)} %param.12) | copy-start | bytes 1179652
  150.6 24.0 %copy-start.7 = (bf16[64,3072]{1,0:T(8,128)(2,1)S(1)}, bf16[64,3072]{1,0:T(8,128)(2,1)}, u32[]{:S(2)}) copy-start(bf16[64,3072]{1,0:T(8,128)(2,1)} %get-tuple-element.62) | copy-start | bytes 1179652
  154.8 12.8 %collective-permute-start.13 = (bf16[64,3072]{1,0:T(8,128)(2,1)S(1)}, bf16[64,3072]{1,0:T(8,128)(2,1)S(1)}, u32[]{:S(2)}, u32[]{:S(2)}) collective-permute-start(bf16[64,3072]{1,0:T(8,128)(2,1)S(1)} %copy-done.18), channel_id=1, source_target_pairs={{0,8},{4,12},{8,16},{12,20},{16,24},{20,28},{24,0},{28,4},{1,9},{5... | collective-permute-start | bytes 1179656 | tf_op jit(solution)/shard_map/ppermute | solution.py:285
  156.0 16.7 %collective-permute-start.14 = (bf16[64,3072]{1,0:T(8,128)(2,1)S(1)}, bf16[64,3072]{1,0:T(8,128)(2,1)S(1)}, u32[]{:S(2)}, u32[]{:S(2)}) collective-permute-start(bf16[64,3072]{1,0:T(8,128)(2,1)S(1)} %copy-done.16), channel_id=1, source_target_pairs={{0,24},{4,28},{8,0},{12,4},{16,8},{20,12},{24,16},{28,20},{1,25},{... | collective-permute-start | bytes 1179656 | tf_op jit(solution)/shard_map/ppermute | solution.py:285
  158.6 16.0 %collective-permute-start.15 = (bf16[64,3072]{1,0:T(8,128)(2,1)S(1)}, bf16[64,3072]{1,0:T(8,128)(2,1)S(1)}, u32[]{:S(2)}, u32[]{:S(2)}) collective-permute-start(bf16[64,3072]{1,0:T(8,128)(2,1)S(1)} %add_convert_fusion.2), channel_id=1, source_target_pairs={{0,16},{4,20},{8,24},{12,28},{16,0},{20,4},{24,8},{28,12},{1,17},{... | collective-permute-start | bytes 1179656 | tf_op jit(solution)/shard_map/ppermute | solution.py:285
  160.0 14.6 %collective-permute-start.16 = (bf16[64,3072]{1,0:T(8,128)(2,1)S(1)}, bf16[64,3072]{1,0:T(8,128)(2,1)S(1)}, u32[]{:S(2)}, u32[]{:S(2)}) collective-permute-start(bf16[64,3072]{1,0:T(8,128)(2,1)S(1)} %add_convert_fusion.3), channel_id=1, source_target_pairs={{0,4},{4,0},{8,12},{12,8},{16,20},{20,16},{24,28},{28,24},{1,5},{5... | collective-permute-start | bytes 1179656 | tf_op jit(solution)/shard_map/ppermute | solution.py:285
  175.3 20.1 %copy-start.2 = (bf16[64,3072]{1,0:T(8,128)(2,1)}, bf16[64,3072]{1,0:T(8,128)(2,1)S(1)}, u32[]{:S(2)}) copy-start(bf16[64,3072]{1,0:T(8,128)(2,1)S(1)} %fusion.6.refs_0_) | copy-start | bytes 1179652
  175.3 9.4 %collective-permute-start.17 = (bf16[64,3072]{1,0:T(8,128)(2,1)S(1)}, bf16[64,3072]{1,0:T(8,128)(2,1)S(1)}, u32[]{:S(2)}, u32[]{:S(2)}) collective-permute-start(bf16[64,3072]{1,0:T(8,128)(2,1)S(1)} %fusion.6.refs_0_), channel_id=1, source_target_pairs={{0,4},{4,0},{8,12},{12,8},{16,20},{20,16},{24,28},{28,24},{1,5},{5... | collective-permute-start | bytes 1179656 | tf_op jit(solution)/shard_map/ppermute | solution.py:285
  177.7 13.6 %collective-permute-start.20 = (bf16[64,3072]{1,0:T(8,128)(2,1)S(1)}, bf16[64,3072]{1,0:T(8,128)(2,1)S(1)}, u32[]{:S(2)}, u32[]{:S(2)}) collective-permute-start(bf16[64,3072]{1,0:T(8,128)(2,1)S(1)} %fusion.6.refs_0_), channel_id=1, source_target_pairs={{0,16},{4,20},{8,24},{12,28},{16,0},{20,4},{24,8},{28,12},{1,17},{... | collective-permute-start | bytes 1179656 | tf_op jit(solution)/shard_map/ppermute | solution.py:285
  178.0 18.4 %collective-permute-start.18 = (bf16[64,3072]{1,0:T(8,128)(2,1)S(1)}, bf16[64,3072]{1,0:T(8,128)(2,1)S(1)}, u32[]{:S(2)}, u32[]{:S(2)}) collective-permute-start(bf16[64,3072]{1,0:T(8,128)(2,1)S(1)} %fusion.6.refs_0_), channel_id=1, source_target_pairs={{0,24},{4,28},{8,0},{12,4},{16,8},{20,12},{24,16},{28,20},{1,25},{... | collective-permute-start | bytes 1179656 | tf_op jit(solution)/shard_map/ppermute | solution.py:285
  181.5 15.9 %collective-permute-start.19 = (bf16[64,3072]{1,0:T(8,128)(2,1)S(1)}, bf16[64,3072]{1,0:T(8,128)(2,1)}, u32[]{:S(2)}, u32[]{:S(2)}) collective-permute-start(bf16[64,3072]{1,0:T(8,128)(2,1)S(1)} %fusion.6.refs_0_), channel_id=1, source_target_pairs={{0,8},{4,12},{8,16},{12,20},{16,24},{20,28},{24,0},{28,4},{1,9},{5... | collective-permute-start | bytes 1179656 | tf_op jit(solution)/shard_map/ppermute | solution.py:285
  184.6 10.7 %copy-start.9 = (bf16[64,3072]{1,0:T(8,128)(2,1)}, bf16[64,3072]{1,0:T(8,128)(2,1)S(1)}, u32[]{:S(2)}) copy-start(bf16[64,3072]{1,0:T(8,128)(2,1)S(1)} %collective-permute-done.17.refs_1_) | copy-start | bytes 1179652
  184.6 22.1 %collective-permute-start.21 = (bf16[64,3072]{1,0:T(8,128)(2,1)S(1)}, bf16[64,3072]{1,0:T(8,128)(2,1)}, u32[]{:S(2)}, u32[]{:S(2)}) collective-permute-start(bf16[64,3072]{1,0:T(8,128)(2,1)S(1)} %collective-permute-done.17.refs_1_), channel_id=1, source_target_pairs={{0,24},{4,28},{8,0},{12,4},{16,8},{20,12},{24,16},{28,20},{1,25},{... | collective-permute-start | bytes 1179656 | tf_op jit(solution)/shard_map/ppermute | solution.py:285
  186.5 20.2 %collective-permute-start.22 = (bf16[64,3072]{1,0:T(8,128)(2,1)S(1)}, bf16[64,3072]{1,0:T(8,128)(2,1)}, u32[]{:S(2)}, u32[]{:S(2)}) collective-permute-start(bf16[64,3072]{1,0:T(8,128)(2,1)S(1)} %collective-permute-done.17.refs_1_), channel_id=1, source_target_pairs={{0,8},{4,12},{8,16},{12,20},{16,24},{20,28},{24,0},{28,4},{1,9},{5... | collective-permute-start | bytes 1179656 | tf_op jit(solution)/shard_map/ppermute | solution.py:285
  191.2 4.1 %copy-start.10 = (bf16[64,3072]{1,0:T(8,128)(2,1)}, bf16[64,3072]{1,0:T(8,128)(2,1)S(1)}, u32[]{:S(2)}) copy-start(bf16[64,3072]{1,0:T(8,128)(2,1)S(1)} %collective-permute-done.20.refs_4_) | copy-start | bytes 1179652
  191.2 15.5 %collective-permute-start.23 = (bf16[64,3072]{1,0:T(8,128)(2,1)S(1)}, bf16[64,3072]{1,0:T(8,128)(2,1)}, u32[]{:S(2)}, u32[]{:S(2)}) collective-permute-start(bf16[64,3072]{1,0:T(8,128)(2,1)S(1)} %collective-permute-done.20.refs_4_), channel_id=1, source_target_pairs={{0,4},{4,0},{8,12},{12,8},{16,20},{20,16},{24,28},{28,24},{1,5},{5... | collective-permute-start | bytes 1179656 | tf_op jit(solution)/shard_map/ppermute | solution.py:285
  196.5 0.8 copy-start.11
  215.8 0.7 collective-permute-start.24
  216.5 0.8 copy-start.24
  218.0 0.7 collective-permute-start.25
  218.7 0.8 copy-start.25
  220.2 16.1 %collective-permute-start.26 = (bf16[2,3,256,128]{3,2,1,0:T(8,128)(2,1)}, bf16[2,3,256,128]{3,2,1,0:T(8,128)(2,1)S(1)}, u32[]{:S(2)}, u32[]{:S(2)}) collective-permute-start(bf16[2,3,256,128]{3,2,1,0:T(8,128)(2,1)} %get-tuple-element.82), channel_id=1, source_target_pairs={{64,96},{65,97},{66,98},{67,99},{68,100},{69,101},{70,102},{71,103... | collective-permute-start | bytes 1179656 | tf_op jit(solution)/shard_map/ppermute | solution.py:334
  236.3 0.8 copy-start.20
  252.2 5.2 %copy-start.6 = (bf16[512,384]{1,0:T(8,128)(2,1)S(1)}, bf16[512,384]{1,0:T(8,128)(2,1)}, u32[]{:S(2)}) copy-start(bf16[512,384]{1,0:T(8,128)(2,1)} %get-tuple-element.84) | copy-start | bytes 1179652
  256.2 9.5 %collective-permute-start.29 = (bf16[64,3072]{1,0:T(8,128)(2,1)}, bf16[64,3072]{1,0:T(8,128)(2,1)S(1)}, u32[]{:S(2)}, u32[]{:S(2)}) collective-permute-start(bf16[64,3072]{1,0:T(8,128)(2,1)} %get-tuple-element.90), channel_id=1, source_target_pairs={{0,4},{4,0},{8,12},{12,8},{16,20},{20,16},{24,28},{28,24},{1,5},{5... | collective-permute-start | bytes 1179656 | tf_op jit(solution)/shard_map/ppermute | solution.py:285
  258.1 12.6 %collective-permute-start.27 = (bf16[64,3072]{1,0:T(8,128)(2,1)}, bf16[64,3072]{1,0:T(8,128)(2,1)S(1)}, u32[]{:S(2)}, u32[]{:S(2)}) collective-permute-start(bf16[64,3072]{1,0:T(8,128)(2,1)} %get-tuple-element.87), channel_id=1, source_target_pairs={{0,8},{4,12},{8,16},{12,20},{16,24},{20,28},{24,0},{28,4},{1,9},{5... | collective-permute-start | bytes 1179656 | tf_op jit(solution)/shard_map/ppermute | solution.py:285
  259.1 12.9 %collective-permute-start.28 = (bf16[64,3072]{1,0:T(8,128)(2,1)}, bf16[64,3072]{1,0:T(8,128)(2,1)S(1)}, u32[]{:S(2)}, u32[]{:S(2)}) collective-permute-start(bf16[64,3072]{1,0:T(8,128)(2,1)} %get-tuple-element.88), channel_id=1, source_target_pairs={{0,24},{4,28},{8,0},{12,4},{16,8},{20,12},{24,16},{28,20},{1,25},{... | collective-permute-start | bytes 1179656 | tf_op jit(solution)/shard_map/ppermute | solution.py:285
  265.6 7.5 %copy-start.19 = (bf16[64,3072]{1,0:T(8,128)(2,1)S(1)}, bf16[64,3072]{1,0:T(8,128)(2,1)}, u32[]{:S(2)}) copy-start(bf16[64,3072]{1,0:T(8,128)(2,1)} %get-tuple-element.93) | copy-start | bytes 1179652
  265.6 9.0 %copy-start.17 = (bf16[64,3072]{1,0:T(8,128)(2,1)S(1)}, bf16[64,3072]{1,0:T(8,128)(2,1)}, u32[]{:S(2)}) copy-start(bf16[64,3072]{1,0:T(8,128)(2,1)} %get-tuple-element.94) | copy-start | bytes 1179652
  265.6 25.5 %copy-start.8 = (bf16[64,3072]{1,0:T(8,128)(2,1)S(1)}, bf16[64,3072]{1,0:T(8,128)(2,1)}, u32[]{:S(2)}) copy-start(bf16[64,3072]{1,0:T(8,128)(2,1)} %get-tuple-element.85) | copy-start | bytes 1179652
  273.1 12.3 %collective-permute-start.30 = (bf16[64,3072]{1,0:T(8,128)(2,1)S(1)}, bf16[64,3072]{1,0:T(8,128)(2,1)S(1)}, u32[]{:S(2)}, u32[]{:S(2)}) collective-permute-start(bf16[64,3072]{1,0:T(8,128)(2,1)S(1)} %copy-done.19), channel_id=1, source_target_pairs={{0,8},{4,12},{8,16},{12,20},{16,24},{20,28},{24,0},{28,4},{1,9},{5... | collective-permute-start | bytes 1179656 | tf_op jit(solution)/shard_map/ppermute | solution.py:285
  274.6 14.6 %collective-permute-start.31 = (bf16[64,3072]{1,0:T(8,128)(2,1)S(1)}, bf16[64,3072]{1,0:T(8,128)(2,1)S(1)}, u32[]{:S(2)}, u32[]{:S(2)}) collective-permute-start(bf16[64,3072]{1,0:T(8,128)(2,1)S(1)} %copy-done.17), channel_id=1, source_target_pairs={{0,24},{4,28},{8,0},{12,4},{16,8},{20,12},{24,16},{28,20},{1,25},{... | collective-permute-start | bytes 1179656 | tf_op jit(solution)/shard_map/ppermute | solution.py:285
  279.8 11.3 %collective-permute-start.32 = (bf16[64,3072]{1,0:T(8,128)(2,1)S(1)}, bf16[64,3072]{1,0:T(8,128)(2,1)S(1)}, u32[]{:S(2)}, u32[]{:S(2)}) collective-permute-start(bf16[64,3072]{1,0:T(8,128)(2,1)S(1)} %add_convert_fusion), channel_id=1, source_target_pairs={{0,16},{4,20},{8,24},{12,28},{16,0},{20,4},{24,8},{28,12},{1,17},{... | collective-permute-start | bytes 1179656 | tf_op jit(solution)/shard_map/ppermute | solution.py:285
  281.2 10.0 %collective-permute-start.33 = (bf16[64,3072]{1,0:T(8,128)(2,1)S(1)}, bf16[64,3072]{1,0:T(8,128)(2,1)S(1)}, u32[]{:S(2)}, u32[]{:S(2)}) collective-permute-start(bf16[64,3072]{1,0:T(8,128)(2,1)S(1)} %add_convert_fusion.1), channel_id=1, source_target_pairs={{0,4},{4,0},{8,12},{12,8},{16,20},{20,16},{24,28},{28,24},{1,5},{5... | collective-permute-start | bytes 1179656 | tf_op jit(solution)/shard_map/ppermute | solution.py:285
